TPU v7x, 32 devices: a whole 2x2x4 slice. The times are simulated.
32 devices in a mesh: batch: 16 (over z, x, core), tensor: 2 (over y).
Axes of the slice: x: 2, y: 2, z: 4, core: 2. Of those that a mesh axis runs over, the one named last changes fastest.
Arguments:
- tokens: bfloat16 [9216, 768], P('batch'), may hold values from -6 to 6
- doc_vectors: bfloat16 [32, 768], P('batch'), may hold values from -3 to 3
- doc_ids: int32 [32], P('batch'), may hold values from 0 to 31, as said below
- w_query: bfloat16 [768, 768], P(None, 'tensor'), may hold values from -0.21875 to 0.21875
- b_query: bfloat16 [768], P('tensor'), may hold values from -2 to 2
- w_key: bfloat16 [768, 768], P(None, 'tensor'), may hold values from -0.21875 to 0.21875
- w_value: bfloat16 [768, 768], P(None, 'tensor'), may hold values from -0.21875 to 0.21875
- b_value: bfloat16 [768], P('tensor'), may hold values from -2 to 2
- w_out: bfloat16 [768, 768], P('tensor'), may hold values from -1.25 to 1.25
- b_out: bfloat16 [768], replicated, may hold values from -2 to 2
- gain_one: bfloat16 [768], replicated, may hold values from 0.25 to 1.75
- shift_one: bfloat16 [768], replicated, may hold values from -2 to 2
- w_inner: bfloat16 [768, 3072], P(None, 'tensor'), may hold values from -0.21875 to 0.21875
- b_inner: bfloat16 [3072], P('tensor'), may hold values from -2 to 2
- w_outer: bfloat16 [3072, 768], P('tensor'), may hold values from -0.109375 to 0.109375
- b_outer: bfloat16 [768], replicated, may hold values from -2 to 2
- gain_two: bfloat16 [768], replicated, may hold values from 0.25 to 1.75
- shift_two: bfloat16 [768], replicated, may hold values from -2 to 2
- cotangent: bfloat16 [9216, 768], P('batch'), may hold values from -6 to 6
Outputs:
- mixed: bfloat16 [9216, 768], P('batch')
- tokens_grad: bfloat16 [9216, 768], P('batch')
- doc_grad: float32 [32, 768], P('batch')
- w_query_grad: float32 [768, 768], P('batch', 'tensor')
- b_query_grad: float32 [768], P(('tensor', 'batch'))
- w_key_grad: float32 [768, 768], P('batch', 'tensor')
- w_value_grad: float32 [768, 768], P('batch', 'tensor')
- b_value_grad: float32 [768], P(('tensor', 'batch'))
- w_out_grad: float32 [768, 768], P('tensor', 'batch')
- b_out_grad: float32 [768], P('batch')
- gain_one_grad: float32 [768], P('batch')
- shift_one_grad: float32 [768], P('batch')
- w_inner_grad: float32 [768, 3072], P('batch', 'tensor')
- b_inner_grad: float32 [3072], P(('tensor', 'batch'))
- w_outer_grad: float32 [3072, 768], P('tensor', 'batch')
- b_outer_grad: float32 [768], P('batch')
- gain_two_grad: float32 [768], P('batch')
- shift_two_grad: float32 [768], P('batch')
Inputs may be any that keep to these rules, and one draw needn't show every extreme that they name: `doc_ids`: the first pair on every index of batch names one common document; the last pair names document 32 - 1.
All inputs are finite; a program needn't handle non-finite values.
Results may differ from a plain program's by a relative error of at most 0.017.
The roundings to bfloat16 on the way count: a program that leaves them out, or rounds other values in their place, can miss the bound.
Values may be sent and summed in bfloat16 or wider, within the bound.
A program may use at most 128 MiB of HBM per device.

v0:
```python
import math

import jax
import jax.numpy as jnp
from jax import lax
from jax.sharding import PartitionSpec as P

HEAD_DIM = 64
QLEN = 32


epsilon = 1e-12


def product(left, right):
    return jnp.dot(left, right, preferred_element_type=jnp.float32)


def normalize(summed, gain, shift):
    centre = jnp.mean(summed, axis=-1, keepdims=True)
    centered = summed - centre
    inverse = lax.rsqrt(jnp.mean(centered * centered, axis=-1, keepdims=True) + epsilon)
    normed = centered * inverse
    return (normed * gain.astype(jnp.float32) + shift.astype(jnp.float32), normed, inverse)


def normalize_back(upstream, gain, normed, inverse):
    scaled = upstream * gain.astype(jnp.float32)
    return inverse * (
        scaled
        - jnp.mean(scaled, axis=-1, keepdims=True)
        - normed * jnp.mean(scaled * normed, axis=-1, keepdims=True)
    )


def gelu_slope(inner):
    normal_cdf = 0.5 * (1.0 + jax.scipy.special.erf(inner * (1.0 / math.sqrt(2.0))))
    density = jnp.exp(-0.5 * inner * inner) * (1.0 / math.sqrt(2.0 * math.pi))
    return normal_cdf + inner * density


def body(
    tokens,
    doc_vectors,
    doc_ids,
    w_query,
    b_query,
    w_key,
    w_value,
    b_value,
    w_out,
    b_out,
    gain_one,
    shift_one,
    w_inner,
    b_inner,
    w_outer,
    b_outer,
    gain_two,
    shift_two,
    cotangent,
):
    pair_count = doc_ids.shape[0]
    row_count, width = tokens.shape
    seq_len = row_count // pair_count
    local_width = w_query.shape[1]
    head_count = local_width // HEAD_DIM
    score_scale = HEAD_DIM ** (-0.5)
    head_shape = (pair_count, seq_len, head_count, HEAD_DIM)
    doc_table = lax.all_gather(doc_vectors, "batch", axis=0, tiled=True)
    doc_numbers = jnp.arange(doc_table.shape[0], dtype=jnp.int32)
    selector = (doc_ids[:, None] == doc_numbers[None, :]).astype(jnp.bfloat16)
    doc_rows = product(selector, doc_table)
    doc_mask = (jnp.arange(seq_len) >= QLEN).astype(jnp.float32)[None, :, None]
    inputs = (
        tokens.astype(jnp.float32).reshape(pair_count, seq_len, width)
        + doc_mask * doc_rows[:, None, :]
    ).reshape(row_count, width)
    inputs_low = inputs.astype(jnp.bfloat16)
    queries = (product(inputs_low, w_query) + b_query.astype(jnp.float32)).astype(jnp.bfloat16)
    keys_low = product(inputs_low, w_key).astype(jnp.bfloat16)
    values_low = (product(inputs_low, w_value) + b_value.astype(jnp.float32)).astype(jnp.bfloat16)
    query_heads = queries.reshape(head_shape)
    key_heads = keys_low.reshape(head_shape)
    value_heads = values_low.reshape(head_shape)
    scores = (
        jnp.einsum("gqhe,gkhe->ghqk", query_heads, key_heads, preferred_element_type=jnp.float32)
        * score_scale
    )
    row_max = jnp.max(scores, axis=-1, keepdims=True)
    expo = jnp.exp(scores - row_max)
    row_total = jnp.sum(expo, axis=-1, keepdims=True)
    probs = expo / row_total
    log_total = row_max + jnp.log(row_total)
    attended = jnp.einsum(
        "ghqk,gkhe->gqhe",
        probs.astype(jnp.bfloat16),
        value_heads,
        preferred_element_type=jnp.float32,
    )
    attended_low = attended.reshape(row_count, local_width).astype(jnp.bfloat16)
    attn_part = product(attended_low, w_out)
    attn_out = lax.psum(attn_part, "tensor") + b_out.astype(jnp.float32)
    upstream = cotangent.astype(jnp.float32)
    hidden_one, normed_one, inverse_one = normalize(inputs + attn_out, gain_one, shift_one)
    hidden_low = hidden_one.astype(jnp.bfloat16)
    inner = product(hidden_low, w_inner) + b_inner.astype(jnp.float32)
    activated = jax.nn.gelu(inner, approximate=False).astype(jnp.bfloat16)
    outer_part = product(activated, w_outer)
    outer = lax.psum(outer_part.astype(jnp.bfloat16), "tensor").astype(
        jnp.float32
    ) + b_outer.astype(jnp.float32)
    result, normed_two, inverse_two = normalize(hidden_one + outer, gain_two, shift_two)
    grad_gain_two = jnp.sum(upstream * normed_two, axis=0)
    grad_shift_two = jnp.sum(upstream, axis=0)
    grad_sum_two = normalize_back(upstream, gain_two, normed_two, inverse_two)
    grad_b_outer = jnp.sum(grad_sum_two, axis=0)
    mixed = result.astype(jnp.bfloat16)
    grad_outer_low = grad_sum_two.astype(jnp.bfloat16)
    grad_w_outer = jnp.einsum(
        "tf,td->fd", activated, grad_outer_low, preferred_element_type=jnp.float32
    )
    grad_activated = jnp.einsum(
        "td,fd->tf", grad_outer_low, w_outer, preferred_element_type=jnp.float32
    )
    grad_inner_low = (grad_activated * gelu_slope(inner)).astype(jnp.bfloat16)
    grad_b_inner = jnp.sum(grad_inner_low.astype(jnp.float32), axis=0)
    grad_w_inner = jnp.einsum(
        "td,tf->df", hidden_low, grad_inner_low, preferred_element_type=jnp.float32
    )
    grad_hidden_part = jnp.einsum(
        "tf,df->td", grad_inner_low, w_inner, preferred_element_type=jnp.float32
    )
    grad_hidden = grad_sum_two + lax.psum(grad_hidden_part, "tensor")
    grad_gain_one = jnp.sum(grad_hidden * normed_one, axis=0)
    grad_shift_one = jnp.sum(grad_hidden, axis=0)
    grad_sum_one = normalize_back(grad_hidden, gain_one, normed_one, inverse_one)
    grad_b_out = jnp.sum(grad_sum_one, axis=0)
    grad_out_low = grad_sum_one.astype(jnp.bfloat16)
    grad_w_out = jnp.einsum(
        "tc,td->cd", attended_low, grad_out_low, preferred_element_type=jnp.float32
    )
    grad_attended = jnp.einsum("td,cd->tc", grad_out_low, w_out, preferred_element_type=jnp.float32)
    grad_attended_heads = grad_attended.astype(jnp.bfloat16).reshape(head_shape)
    scores_again = (
        jnp.einsum("gqhe,gkhe->ghqk", query_heads, key_heads, preferred_element_type=jnp.float32)
        * score_scale
    )
    probs_again = jnp.exp(scores_again - log_total)
    grad_values = jnp.einsum(
        "ghqk,gqhe->gkhe",
        probs_again.astype(jnp.bfloat16),
        grad_attended_heads,
        preferred_element_type=jnp.float32,
    ).astype(jnp.bfloat16)
    grad_probs = jnp.einsum(
        "gqhe,gkhe->ghqk", grad_attended_heads, value_heads, preferred_element_type=jnp.float32
    )
    grad_scores = probs_again * (
        grad_probs - jnp.sum(probs_again * grad_probs, axis=-1, keepdims=True)
    )
    grad_scores_low = grad_scores.astype(jnp.bfloat16)
    grad_queries = (
        (
            jnp.einsum(
                "ghqk,gkhe->gqhe", grad_scores_low, key_heads, preferred_element_type=jnp.float32
            )
            * score_scale
        )
        .astype(jnp.bfloat16)
        .reshape(row_count, local_width)
    )
    grad_keys = (
        (
            jnp.einsum(
                "ghqk,gqhe->gkhe", grad_scores_low, query_heads, preferred_element_type=jnp.float32
            )
            * score_scale
        )
        .astype(jnp.bfloat16)
        .reshape(row_count, local_width)
    )
    grad_values = grad_values.reshape(row_count, local_width)
    grad_w_query = jnp.einsum(
        "td,tc->dc", inputs_low, grad_queries, preferred_element_type=jnp.float32
    )
    grad_b_query = jnp.sum(grad_queries.astype(jnp.float32), axis=0)
    grad_w_key = jnp.einsum("td,tc->dc", inputs_low, grad_keys, preferred_element_type=jnp.float32)
    grad_w_value = jnp.einsum(
        "td,tc->dc", inputs_low, grad_values, preferred_element_type=jnp.float32
    )
    grad_b_value = jnp.sum(grad_values.astype(jnp.float32), axis=0)
    input_part = (
        jnp.einsum("tc,dc->td", grad_queries, w_query, preferred_element_type=jnp.float32)
        + jnp.einsum("tc,dc->td", grad_keys, w_key, preferred_element_type=jnp.float32)
        + jnp.einsum("tc,dc->td", grad_values, w_value, preferred_element_type=jnp.float32)
    )
    input_grad = grad_sum_one + lax.psum(input_part.astype(jnp.bfloat16), "tensor").astype(
        jnp.float32
    )
    tokens_grad = input_grad.astype(jnp.bfloat16)
    doc_sums = jnp.sum(input_grad.reshape(pair_count, seq_len, width) * doc_mask, axis=1)
    doc_part = jnp.einsum(
        "pn,pd->nd", selector.astype(jnp.float32), doc_sums, precision=lax.Precision.HIGHEST
    )
    (
        out_doc,
        out_query_w,
        out_query_b,
        out_key_w,
        out_value_w,
        out_value_b,
        out_out_w,
        out_out_b,
        out_gain_one,
        out_shift_one,
        late_inner_w,
        late_inner_b,
        late_outer_w,
        late_outer_b,
        late_gain_two,
        late_shift_two,
    ) = (
        lax.psum_scatter(doc_part, "batch", scatter_dimension=0, tiled=True),
        lax.psum_scatter(grad_w_query, "batch", scatter_dimension=0, tiled=True),
        lax.psum_scatter(grad_b_query, "batch", scatter_dimension=0, tiled=True),
        lax.psum_scatter(grad_w_key, "batch", scatter_dimension=0, tiled=True),
        lax.psum_scatter(grad_w_value, "batch", scatter_dimension=0, tiled=True),
        lax.psum_scatter(grad_b_value, "batch", scatter_dimension=0, tiled=True),
        lax.psum_scatter(grad_w_out, "batch", scatter_dimension=1, tiled=True),
        lax.psum_scatter(grad_b_out, "batch", scatter_dimension=0, tiled=True),
        lax.psum_scatter(grad_gain_one, "batch", scatter_dimension=0, tiled=True),
        lax.psum_scatter(grad_shift_one, "batch", scatter_dimension=0, tiled=True),
        lax.psum_scatter(grad_w_inner, "batch", scatter_dimension=0, tiled=True),
        lax.psum_scatter(grad_b_inner, "batch", scatter_dimension=0, tiled=True),
        lax.psum_scatter(grad_w_outer, "batch", scatter_dimension=1, tiled=True),
        lax.psum_scatter(grad_b_outer, "batch", scatter_dimension=0, tiled=True),
        lax.psum_scatter(grad_gain_two, "batch", scatter_dimension=0, tiled=True),
        lax.psum_scatter(grad_shift_two, "batch", scatter_dimension=0, tiled=True),
    )
    return (
        mixed,
        tokens_grad,
        out_doc,
        out_query_w,
        out_query_b,
        out_key_w,
        out_value_w,
        out_value_b,
        out_out_w,
        out_out_b,
        out_gain_one,
        out_shift_one,
        late_inner_w,
        late_inner_b,
        late_outer_w,
        late_outer_b,
        late_gain_two,
        late_shift_two,
    )


def solution(mesh):
    in_specs = (
        P("batch", None),
        P("batch", None),
        P("batch"),
        P(None, "tensor"),
        P("tensor"),
        P(None, "tensor"),
        P(None, "tensor"),
        P("tensor"),
        P("tensor", None),
        P(),
        P(),
        P(),
        P(None, "tensor"),
        P("tensor"),
        P("tensor", None),
        P(),
        P(),
        P(),
        P("batch", None),
    )
    out_specs = (
        P("batch", None),
        P("batch", None),
        P("batch", None),
        P("batch", "tensor"),
        P(("tensor", "batch")),
        P("batch", "tensor"),
        P("batch", "tensor"),
        P(("tensor", "batch")),
        P("tensor", "batch"),
        P("batch"),
        P("batch"),
        P("batch"),
        P("batch", "tensor"),
        P(("tensor", "batch")),
        P("tensor", "batch"),
        P("batch"),
        P("batch"),
        P("batch"),
    )
    return jax.shard_map(body, mesh=mesh, in_specs=in_specs, out_specs=out_specs, check_vma=False)
```

profile of v0, /device:TPU:0, one launch (start us, length us, event | category | flops | bytes accessed | tf_op | source)
XLA Modules:
  0.0 834.8 jit_solution(160932060678638452)
XLA Ops:
  7.3 23.5 %all-gather = bf16[16,2,768]{2,1,0:T(2,128)(2,1)S(1)} all-gather(bf16[1,2,768]{2,1,0:T(2,128)(2,1)} %bitcast.72), channel_id=1, replica_groups=mesh['batch'=16,'tensor'=2] {'batch'}, dimensions={0}, use_global_device_ids=true | all-gather | bytes 52224 | tf_op jit(solution)/shard_map/all_gather | solution.py:70
  62.9 2.7 convert_element_type.152
  65.6 3.2 fusion.69
  69.1 52.9 %all-reduce.17.cloned.1.call-done = f32[576,768]{1,0:T(8,128)} async-done(((f32[576,768]{1,0:T(8,128)}), f32[576,768]{1,0:T(8,128)}) %all-reduce.17.cloned.1.call-update) | async-done | bytes 1769488 | tf_op jit(solution)/shard_map/psum | solution.py:103
  122.1 3.3 add_add_fusion.1
  128.9 11.3 %fusion.3 = (bf16[576,1536]{1,0:T(8,128)(2,1)S(1)}, f32[576,1536]{1,0:T(8,128)}) fusion(f32[1536]{0:T(1024)S(1)} %convert_element_type.157, bf16[768,1536]{1,0:T(8,128)(2,1)S(1)} %copy-done, f32[576,768]{1,0:T(8,128)} %add_add_fusion.1, f32[768]{0:T(1024)S(1)} %convert_element_type.155, f32[768]{0:T(1024)S(1)} %convert_element_type.154, ...), kind=kOutput, calls=%fused_computation.11 | convolution fusion | flops 1419558912 | bytes 9454080 | tf_op jit(solution)/shard_map/dot_general | solution.py:16
  144.0 36.5 %all-reduce.19.cloned.1.call-done = bf16[576,768]{1,0:T(8,128)(2,1)} async-done(((bf16[576,768]{1,0:T(8,128)(2,1)}), bf16[576,768]{1,0:T(8,128)(2,1)}) %all-reduce.19.cloned.1.call-update) | async-done | bytes 884752 | tf_op jit(solution)/shard_map/psum | solution.py:110
  186.5 3.0 convert_reduce_fusion
  190.8 2.8 fusion.70
  193.6 55.9 %all-reduce.21.cloned.1.call-done = f32[576,768]{1,0:T(8,128)} async-done(((f32[576,768]{1,0:T(8,128)}), f32[576,768]{1,0:T(8,128)}) %all-reduce.21.cloned.1.call-update) | async-done | bytes 1769488 | tf_op jit(solution)/shard_map/psum | solution.py:134
  249.5 3.6 multiply_reduce_fusion.2
  261.5 4.0 convert_reduce_fusion.2
  265.5 4.0 multiply_reduce_fusion
  275.7 2.7 reshape.141
  280.9 2.7 reshape.140
  283.7 3.1 fusion.72
  288.2 2.9 reshape.139
  294.9 36.6 %all-reduce.23.cloned.1.call-done = bf16[576,768]{1,0:T(8,128)(2,1)} async-done(((bf16[576,768]{1,0:T(8,128)(2,1)}), bf16[576,768]{1,0:T(8,128)(2,1)}) %all-reduce.23.cloned.1.call-update) | async-done | bytes 884752 | tf_op jit(solution)/shard_map/psum | solution.py:198
  331.5 2.8 fusion.67
  335.5 2.8 fusion.75
  338.5 2.8 fusion.74
  341.4 3.5 fusion.47
  344.9 2.9 fusion.73
  347.9 6.4 fusion.60
  354.3 6.2 fusion.50
  364.6 61.2 %all-reduce.10 = (f32[384]{0:T(512)S(1)}, f32[384]{0:T(512)S(1)}, f32[768]{0:T(1024)S(1)}, f32[768]{0:T(1024)S(1)}, f32[768]{0:T(1024)S(1)}, /*index=5*/f32[1536...) all-reduce(f32[384]{0:T(512)S(1)} %reduce_sum.196, ...), channel_id=4, replica_groups=mesh['batch'=16,'tensor'=2] {'batch'}, use_global_device_ids=true, to_apply=%region_19.0.clone | all-reduce | flops 6912 | bytes 55296
  432.3 51.9 %reduce-scatter.11.cloned.1.call-done = f32[48,384]{1,0:T(8,128)} async-done(((f32[768,384]{1,0:T(8,128)}), f32[48,384]{1,0:T(8,128)}) %reduce-scatter.11.cloned.1.call-update) | async-done | bytes 73744 | tf_op jit(solution)/shard_map/reduce_scatter | solution.py:228
  484.2 61.8 %reduce-scatter.9.cloned.1.call-done = f32[48,384]{1,0:T(8,128)} async-done(((f32[768,384]{1,0:T(8,128)}), f32[48,384]{1,0:T(8,128)}) %reduce-scatter.9.cloned.1.call-update) | async-done | bytes 73744 | tf_op jit(solution)/shard_map/reduce_scatter | solution.py:227
  546.0 61.7 %reduce-scatter.13.cloned.1.call-done = f32[384,48]{0,1:T(8,128)} async-done(((f32[384,768]{0,1:T(8,128)}), f32[384,48]{0,1:T(8,128)}) %reduce-scatter.13.cloned.1.call-update) | async-done | bytes 73744 | tf_op jit(solution)/shard_map/reduce_scatter | solution.py:230
  607.7 61.7 %reduce-scatter.7.cloned.1.call-done = f32[48,384]{1,0:T(8,128)} async-done(((f32[768,384]{1,0:T(8,128)}), f32[48,384]{1,0:T(8,128)}) %reduce-scatter.7.cloned.1.call-update) | async-done | bytes 73744 | tf_op jit(solution)/shard_map/reduce_scatter | solution.py:225
  669.4 79.3 %reduce-scatter.15.cloned.1.call-done = f32[48,1536]{1,0:T(8,128)} async-done(((f32[768,1536]{1,0:T(8,128)}), f32[48,1536]{1,0:T(8,128)}) %reduce-scatter.15.cloned.1.call-update) | async-done | bytes 294928 | tf_op jit(solution)/shard_map/reduce_scatter | solution.py:234
  748.7 79.1 %reduce-scatter.17.cloned.1.call-done = f32[1536,48]{0,1:T(8,128)} async-done(((f32[1536,768]{0,1:T(8,128)}), f32[1536,48]{0,1:T(8,128)}) %reduce-scatter.17.cloned.1.call-update) | async-done | bytes 294928 | tf_op jit(solution)/shard_map/reduce_scatter | solution.py:236
  (160 shorter events, 78.2 us)
Async XLA Ops:
  7.2 121.7 %copy-start = (bf16[768,1536]{1,0:T(8,128)(2,1)S(1)}, bf16[768,1536]{1,0:T(8,128)(2,1)}, u32[]{:S(2)}) copy-start(bf16[768,1536]{1,0:T(8,128)(2,1)} %param.31) | copy-start | bytes 7077892
  7.2 114.9 %all-reduce.17.cloned.1.call-start = ((), (), s32[]{:S(2)}) async-start(), calls=%async_computation.6 | async-start | bytes 3538944 | tf_op jit(solution)/shard_map/psum | solution.py:103
  41.2 7.3 copy-start.23
  57.9 2.3 copy-start.1
  65.6 3.5 copy-start.17
  65.6 3.5 copy-start.18
  65.6 3.5 copy-start.19
  65.6 3.5 copy-start.16
  68.8 111.7 %all-reduce.19.cloned.1.call-start = ((), (), s32[]{:S(2)}) async-start(), calls=%async_computation.7 | async-start | bytes 1769472 | tf_op jit(solution)/shard_map/psum | solution.py:110
  128.9 12.5 %copy-start.25 = (bf16[1536,768]{1,0:T(8,128)(2,1)S(1)}, bf16[1536,768]{1,0:T(8,128)(2,1)}, u32[]{:S(2)}) copy-start(bf16[1536,768]{1,0:T(8,128)(2,1)} %param.33) | copy-start | bytes 7077892
  141.4 2.5 copy-start.20
  141.4 2.6 copy-start.21
  141.4 2.6 copy-start.22
  143.9 105.6 %all-reduce.21.cloned.1.call-start = ((), (), s32[]{:S(2)}) async-start(), calls=%async_computation.8 | async-start | bytes 3538944 | tf_op jit(solution)/shard_map/psum | solution.py:134
  180.5 2.9 copy-start.10
  183.4 2.6 copy-start.30
  186.0 3.6 copy-start.4
  193.6 137.9 %all-reduce.23.cloned.1.call-start = ((), (), s32[]{:S(2)}) async-start(), calls=%async_computation.9 | async-start | bytes 1769472 | tf_op jit(solution)/shard_map/psum | solution.py:198
  249.5 3.6 copy-start.2
  261.5 4.0 copy-start.7
  261.5 4.0 copy-start.12
  261.5 8.1 slice-start
  265.5 4.1 slice-start.1
  283.7 3.2 copy-start.13
  294.9 39.7 %copy-start.24 = (s32[2]{0:T(128)S(1)}, s32[2]{0:T(128)}, u32[]{:S(2)}) copy-start(s32[2]{0:T(128)} %param.21) | copy-start | bytes 28
  294.9 136.1 %all-reduce.25.cloned.1.call-start = ((), (), s32[]{:S(2)}) async-start(), calls=%async_computation.16 | async-start | bytes 196608
  335.5 148.7 %reduce-scatter.11.cloned.1.call-start = ((), (), s32[]{:S(2)}) async-start(), calls=%async_computation.12 | async-start | bytes 1253376 | tf_op jit(solution)/shard_map/reduce_scatter | solution.py:228
  338.4 207.6 %reduce-scatter.9.cloned.1.call-start = ((), (), s32[]{:S(2)}) async-start(), calls=%async_computation.11 | async-start | bytes 1253376 | tf_op jit(solution)/shard_map/reduce_scatter | solution.py:227
  341.3 266.4 %reduce-scatter.13.cloned.1.call-start = ((), (), s32[]{:S(2)}) async-start(), calls=%async_computation.13 | async-start | bytes 1253376 | tf_op jit(solution)/shard_map/reduce_scatter | solution.py:230
  344.9 324.5 %reduce-scatter.7.cloned.1.call-start = ((), (), s32[]{:S(2)}) async-start(), calls=%async_computation.10 | async-start | bytes 1253376 | tf_op jit(solution)/shard_map/reduce_scatter | solution.py:225
  347.8 400.9 %reduce-scatter.15.cloned.1.call-start = ((), (), s32[]{:S(2)}) async-start(), calls=%async_computation.14 | async-start | bytes 5013504 | tf_op jit(solution)/shard_map/reduce_scatter | solution.py:234
  354.3 473.5 %reduce-scatter.17.cloned.1.call-start = ((), (), s32[]{:S(2)}) async-start(), calls=%async_computation.15 | async-start | bytes 5013504 | tf_op jit(solution)/shard_map/reduce_scatter | solution.py:236
  (12 other events, 19.8 us)
Sparse Core Ops, SparseCore 0:
  69.0 53.0 all-reduce.16
  144.0 36.4 all-reduce.18
  193.7 55.7 all-reduce.20
  295.0 36.4 all-reduce.22
  335.6 87.0 all-reduce.24
  427.2 56.9 reduce-scatter.10
  488.8 57.0 reduce-scatter.8
  550.6 57.0 reduce-scatter.12
  612.3 57.0 reduce-scatter.6
  674.2 74.5 reduce-scatter.14
  753.2 74.5 reduce-scatter.16
where the time goes:
time: 843 us; the launch traced here: 835 us
  waiting for transfers between devices  578 us (69%)
  blocking collectives  84.7 us (10%)
  matrix products  79.5 us (9%)
  local copies, waits for them, and re-layouts  51.1 us (6%)
  other arithmetic  23.8 us (3%)
  between operations  17.5 us (2%)
    reduce_scatter x1, waiting for transfers between devices, body(): lax.psum_scatter(grad_w_inner, 'batch', scatter_dimension=0, tiled=True)  79.3 us
    reduce_scatter x1, waiting for transfers between devices, body(): lax.psum_scatter(grad_w_outer, 'batch', scatter_dimension=1, tiled=True)  79.1 us
    reduce_scatter x1, waiting for transfers between devices, body(): lax.psum_scatter(grad_w_key, 'batch', scatter_dimension=0, tiled=True)  61.8 us
    reduce_scatter x1, waiting for transfers between devices, body(): lax.psum_scatter(grad_w_query, 'batch', scatter_dimension=0, tiled=True)  61.7 us
    reduce_scatter x1, waiting for transfers between devices, body(): lax.psum_scatter(grad_w_out, 'batch', scatter_dimension=1, tiled=True)  61.7 us
    unnamed x1, blocking collectives  61.2 us
    psum x1, waiting for transfers between devices, body(): grad_hidden = grad_sum_two + lax.psum(grad_hidden_part, 'tensor')  55.9 us
    psum x1, waiting for transfers between devices, body(): attn_out = lax.psum(attn_part, 'tensor') + b_out.astype(jnp.float32)  52.9 us
  transfers between devices with their start and end apart: 11, of which 10 were waited for; matrix products, arithmetic and copies ran while one was open for 4% of the time, Pallas kernels for 0%

commit v1 on v0

v1 whole, which is shorter than its diff:
```python
import functools
import math

import jax
import jax.numpy as jnp
from jax import lax
from jax.experimental import pallas as pl
from jax.experimental.pallas import tpu as pltpu
from jax.sharding import PartitionSpec as P

HEAD_DIM = 64
QLEN = 32
LANES = 128
GROUP = 16
EPSILON = 1e-12
F32 = jnp.float32
BF16 = jnp.bfloat16
MESH = pl.DeviceIdType.MESH

ROW_BQ, ROW_BV, ROW_BOUT, ROW_G1, ROW_S1, ROW_BIN, ROW_BOUTER, ROW_G2, ROW_S2 = range(9)
SMALL_ROWS = 16


def product(left, right, left_dim=1, right_dim=0):
    return lax.dot_general(
        left, right, (((left_dim,), (right_dim,)), ((), ())), preferred_element_type=F32
    )


def fold_rows(block):
    return jnp.sum(block.reshape(block.shape[0] // 8, 8, block.shape[1]), axis=0)


def row_mean(block):
    return jnp.mean(block, axis=1, keepdims=True)


def layer_kernel(
    sizes,
    tokens_hbm, cot_hbm, wq_hbm, wk_hbm, wv_hbm, wo_hbm, wi_hbm, w2_hbm,
    docs_ref, ids_ref, bq_ref, bv_ref, bo_ref, g1_ref, s1_ref, bi_ref, b2_ref, g2_ref, s2_ref,
    mixed_hbm, tgrad_hbm, grads_out, small_out, docs_out,
    tok, cot, wq, wk, wv, wo, wi, w2,
    x_low, q_s, k_s, v_s, p_s, att, n1_s, r1_s, h1_low, g_s, sl_s, dz_s, df_s, du_s,
    da_s, dq_s, dk_s, dv_s, out_s, acc, accb, accq, bin_s,
    y_send, y_recv, sb, rb0, rb1, rb2, ss, rs0, rs1, rs2,
    doc_stage, doc_table, doc_part, doc_in,
    y_ssem, y_rsem, r_ssem, r_rsem, d_ssem, d_rsem, load_sem, out_sem,
):
    n_batch, pairs, seq = sizes
    rows, width = tok.shape
    local = wq.shape[1]
    hidden = wi.shape[1]
    chunk = width // GROUP
    docs_dev = docs_ref.shape[0]
    doc_cols = width // LANES
    inner = n_batch // GROUP

    b = lax.axis_index("batch")
    t = lax.axis_index("tensor")
    place = b // inner
    rest = b % inner
    core = place % 2
    xpos = (place // 2) % 2
    zpos = place // 4
    zs = GROUP // 4

    def at_place(other):
        return (other * inner + rest, t)

    y_peer = (b, 1 - t)
    core_peer = at_place(place + 1 - 2 * core)
    x_peer = at_place(place + 2 - 4 * xpos)

    def z_peer(step):
        return at_place(((zpos + step) % zs) * 4 + xpos * 2 + core)

    def batch_peer(step):
        return ((b + step) % n_batch, t)

    loads = []
    for i, (src, dst) in enumerate(
        (
            (tokens_hbm, tok), (wq_hbm, wq), (wk_hbm, wk), (wv_hbm, wv),
            (wo_hbm, wo), (wi_hbm, wi), (w2_hbm, w2), (cot_hbm, cot),
        )
    ):
        copy = pltpu.make_async_copy(src, dst, load_sem.at[i])
        copy.start()
        loads.append(copy)
    (tok_load, wq_load, wk_load, wv_load, wo_load, wi_load, w2_load, cot_load) = loads

    barrier = pltpu.get_barrier_semaphore()

    def greet(step, carry):
        pl.semaphore_signal(barrier, inc=1, device_id=batch_peer(step), device_id_type=MESH)
        return carry

    lax.fori_loop(1, n_batch, greet, 0)
    pl.semaphore_signal(barrier, inc=1, device_id=y_peer, device_id_type=MESH)

    doc_rows = docs_ref[...].astype(F32)
    pieces = []
    for n in range(docs_dev):
        for j in range(8):
            if j < doc_cols:
                pieces.append(doc_rows[n : n + 1, j * LANES : (j + 1) * LANES])
            else:
                pieces.append(jnp.zeros((1, LANES), F32))
    stage = jnp.concatenate(pieces, axis=0).astype(BF16)
    doc_stage[...] = stage
    doc_table[b] = stage

    bq = bq_ref[...].astype(F32).reshape(1, local)
    bv = bv_ref[...].astype(F32).reshape(1, local)
    b_out = bo_ref[...].astype(F32).reshape(1, width)
    gain1 = g1_ref[...].astype(F32).reshape(1, width)
    shift1 = s1_ref[...].astype(F32).reshape(1, width)
    bin_s[...] = bi_ref[...].astype(F32).reshape(1, hidden)
    b_outer = b2_ref[...].astype(F32).reshape(1, width)
    gain2 = g2_ref[...].astype(F32).reshape(1, width)
    shift2 = s2_ref[...].astype(F32).reshape(1, width)

    pl.semaphore_wait(barrier, n_batch)

    def doc_copy(step):
        return pltpu.make_async_remote_copy(
            src_ref=doc_stage,
            dst_ref=doc_table.at[b],
            send_sem=d_ssem.at[0, step],
            recv_sem=d_rsem.at[0, b],
            device_id=batch_peer(step),
            device_id_type=MESH,
        )

    def doc_arrival(step):
        other = (b + step) % n_batch
        return pltpu.make_async_remote_copy(
            src_ref=doc_stage,
            dst_ref=doc_table.at[other],
            send_sem=d_ssem.at[0, step],
            recv_sem=d_rsem.at[0, other],
            device_id=batch_peer(step),
            device_id_type=MESH,
        )

    def doc_start(step, carry):
        doc_copy(step).start()
        return carry

    def doc_wait(step, carry):
        doc_arrival(step).wait_recv()
        return carry

    def doc_sent(step, carry):
        doc_copy(step).wait_send()
        return carry

    lax.fori_loop(1, n_batch, doc_start, 0)
    tok_load.wait()
    lax.fori_loop(1, n_batch, doc_wait, 0)

    ids = [jnp.full((8, LANES), ids_ref[p], jnp.int32) for p in range(pairs)]

    def pick(d, found):
        block = doc_table[d].astype(F32)
        result = []
        for p in range(pairs):
            value = found[p]
            for n in range(docs_dev):
                value = value + jnp.where(
                    ids[p] == d * docs_dev + n, block[8 * n : 8 * n + 8, :], 0.0
                )
            result.append(value)
        return tuple(result)

    found = lax.fori_loop(
        0, n_batch, pick, tuple(jnp.zeros((8, LANES), F32) for _ in range(pairs))
    )
    doc_row = [
        jnp.concatenate([found[p][j : j + 1, :] for j in range(doc_cols)], axis=1)
        for p in range(pairs)
    ]

    def pair_rows(p):
        return pl.ds(p * seq, seq)

    def blocks(size):
        return seq // size

    def inputs_of(p, i, size):
        base = pl.multiple_of(i * size, size)
        where_row = base + lax.broadcasted_iota(jnp.int32, (size, 1), 0)
        rows_here = pl.ds(pl.multiple_of(p * seq + i * size, 16), size)
        values = tok[rows_here, :].astype(F32) + jnp.where(where_row >= QLEN, doc_row[p], 0.0)
        return rows_here, values

    def y_copy(kind, p):
        return pltpu.make_async_remote_copy(
            src_ref=y_send.at[kind, p],
            dst_ref=y_recv.at[kind, p],
            send_sem=y_ssem.at[kind, p],
            recv_sem=y_rsem.at[kind, p],
            device_id=y_peer,
            device_id_type=MESH,
        )

    def y_sum(kind, p, i, size):
        here = pl.ds(pl.multiple_of(i * size, 16), size)
        return y_send[kind, p, here, :].astype(F32) + y_recv[kind, p, here, :].astype(F32)

    O_SUM, F_SUM, DH_SUM, DX_SUM = range(4)
    first_lanes = lax.broadcasted_iota(jnp.int32, (1, LANES), 1) < HEAD_DIM

    def head_lanes(values, h):
        keep = first_lanes if h == 0 else jnp.logical_not(first_lanes)
        return jnp.where(keep, values, jnp.zeros_like(values))

    def add_acc(which, p, value):
        if p == 0:
            acc[which] = value
        else:
            acc[which] = acc[which] + value

    A_G2, A_S2, A_BOUTER, A_G1, A_S1, A_BOUT = range(6)

    BLOCK = 96

    def make_inputs(p):
        @pl.loop(0, blocks(BLOCK))
        def _(i):
            rows_here, values = inputs_of(p, i, BLOCK)
            x_low[rows_here, :] = values.astype(BF16)

    def attention(p):
        mine = pair_rows(p)
        xl = x_low[mine, :]
        q_s[mine, :] = ((product(xl, wq[...]) + bq).astype(BF16).astype(F32) * 0.125).astype(BF16)
        k_s[mine, :] = product(xl, wk[...]).astype(BF16)
        v_s[mine, :] = (product(xl, wv[...]) + bv).astype(BF16)

        @pl.loop(0, local // LANES)
        def _(j):
            cols = pl.ds(pl.multiple_of(j * LANES, LANES), LANES)
            qq, kk, vv = q_s[mine, cols], k_s[mine, cols], v_s[mine, cols]
            outs = []
            for h in range(2):
                scores = product(head_lanes(qq, h), kk, 1, 1)
                expo = jnp.exp(scores - jnp.max(scores, axis=1, keepdims=True))
                probs = expo * (1.0 / jnp.sum(expo, axis=1, keepdims=True))
                p_s[p * (local // HEAD_DIM) + 2 * j + h] = probs
                outs.append(product(probs.astype(BF16), vv))
            att[mine, cols] = jnp.where(first_lanes, outs[0], outs[1]).astype(BF16)

    def attention_out(p):
        y_send[O_SUM, p] = product(att[pair_rows(p), :], wo[...]).astype(BF16)

    def norm_one(p):
        @pl.loop(0, blocks(BLOCK))
        def _(i):
            rows_here, values = inputs_of(p, i, BLOCK)
            summed = values + (y_sum(O_SUM, p, i, BLOCK) + b_out)
            centered = summed - row_mean(summed)
            inverse = lax.rsqrt(row_mean(centered * centered) + EPSILON)
            normed = centered * inverse
            n1_s[rows_here, :] = normed
            r1_s[rows_here, :] = inverse
            h1_low[rows_here, :] = (normed * gain1 + shift1).astype(BF16)

    FF_TILE = 512

    def feed_forward(p):
        mine = pair_rows(p)

        @pl.loop(0, hidden // FF_TILE)
        def _(j):
            cols = pl.ds(pl.multiple_of(j * FF_TILE, LANES), FF_TILE)
            u = product(h1_low[mine, :], wi[:, cols]) + bin_s[:, cols]
            cdf = 0.5 * (1.0 + lax.erf(u * (1.0 / math.sqrt(2.0))))
            density = jnp.exp(-0.5 * u * u) * (1.0 / math.sqrt(2.0 * math.pi))
            g_s[mine, cols] = (u * cdf).astype(BF16)
            sl_s[mine, cols] = cdf + u * density

        half = width // 2

        @pl.loop(0, 2)
        def _(j):
            cols = pl.ds(pl.multiple_of(j * half, LANES), half)
            y_send[F_SUM, p, :, cols] = product(g_s[mine, :], w2[:, cols]).astype(BF16)

    def norm_two(p):
        def step(i, sums):
            size = BLOCK
            here = pl.ds(pl.multiple_of(p * seq + i * size, 16), size)
            h1 = n1_s[here, :] * gain1 + shift1
            summed = h1 + (y_sum(F_SUM, p, i, size) + b_outer)
            centered = summed - row_mean(summed)
            inverse = lax.rsqrt(row_mean(centered * centered) + EPSILON)
            normed = centered * inverse
            out_s[here, :] = (normed * gain2 + shift2).astype(BF16)
            dy = cot[here, :].astype(F32)
            dyn = dy * normed
            scaled = dy * gain2
            dz = inverse * (scaled - row_mean(scaled) - normed * row_mean(scaled * normed))
            dz_s[here, :] = dz
            df_s[here, :] = dz.astype(BF16)
            return (sums[0] + fold_rows(dyn), sums[1] + fold_rows(dy), sums[2] + fold_rows(dz))

        zero = jnp.zeros((8, width), F32)
        sums = lax.fori_loop(0, blocks(BLOCK), step, (zero, zero, zero))
        add_acc(A_G2, p, sums[0])
        add_acc(A_S2, p, sums[1])
        add_acc(A_BOUTER, p, sums[2])

    def feed_forward_back(p):
        mine = pair_rows(p)

        @pl.loop(0, hidden // FF_TILE)
        def _(j):
            cols = pl.ds(pl.multiple_of(j * FF_TILE, LANES), FF_TILE)
            da = product(df_s[mine, :], w2[cols, :], 1, 1)
            du = (da * sl_s[mine, cols]).astype(BF16)
            du_s[mine, cols] = du
            total = fold_rows(du.astype(F32))
            if p == 0:
                accb[:, cols] = total
            else:
                accb[:, cols] = accb[:, cols] + total

        third = width // 3

        @pl.loop(0, 3)
        def _(j):
            cols = pl.ds(pl.multiple_of(j * third, LANES), third)
            y_send[DH_SUM, p, :, cols] = product(du_s[mine, :], wi[cols, :], 1, 1).astype(BF16)

    def norm_one_back(p):
        def step(i, sums):
            size = BLOCK
            here = pl.ds(pl.multiple_of(p * seq + i * size, 16), size)
            dh = dz_s[here, :] + y_sum(DH_SUM, p, i, size)
            normed = n1_s[here, :]
            scaled = dh * gain1
            dz = r1_s[here, :] * (
                scaled - row_mean(scaled) - normed * row_mean(scaled * normed)
            )
            dz_s[here, :] = dz
            df_s[here, :] = dz.astype(BF16)
            return (
                sums[0] + fold_rows(dh * normed),
                sums[1] + fold_rows(dh),
                sums[2] + fold_rows(dz),
            )

        zero = jnp.zeros((8, width), F32)
        sums = lax.fori_loop(0, blocks(BLOCK), step, (zero, zero, zero))
        add_acc(A_G1, p, sums[0])
        add_acc(A_S1, p, sums[1])
        add_acc(A_BOUT, p, sums[2])

    def attention_back(p):
        mine = pair_rows(p)
        da_s[mine, :] = product(df_s[mine, :], wo[...], 1, 1).astype(BF16)

        @pl.loop(0, local // LANES)
        def _(j):
            cols = pl.ds(pl.multiple_of(j * LANES, LANES), LANES)
            qq, kk, vv, dd = q_s[mine, cols], k_s[mine, cols], v_s[mine, cols], da_s[mine, cols]
            dqs, dks, dvs = [], [], []
            for h in range(2):
                probs = p_s[p * (local // HEAD_DIM) + 2 * j + h]
                dvs.append(product(probs.astype(BF16), dd, 0, 0))
                dp = product(head_lanes(dd, h), vv, 1, 1)
                ds = probs * (dp - jnp.sum(probs * dp, axis=1, keepdims=True))
                ds = ds.astype(BF16)
                dqs.append(product(ds, kk))
                dks.append(product(ds, qq, 0, 0))
            dq_s[mine, cols] = (jnp.where(first_lanes, dqs[0], dqs[1]) * 0.125).astype(BF16)
            dk_s[mine, cols] = jnp.where(first_lanes, dks[0], dks[1]).astype(BF16)
            dv_s[mine, cols] = jnp.where(first_lanes, dvs[0], dvs[1]).astype(BF16)

        total_q = fold_rows(dq_s[mine, :].astype(F32))
        total_v = fold_rows(dv_s[mine, :].astype(F32))
        if p == 0:
            accq[0] = total_q
            accq[1] = total_v
        else:
            accq[0] = accq[0] + total_q
            accq[1] = accq[1] + total_v

    def inputs_back(p):
        mine = pair_rows(p)
        third = width // 3

        @pl.loop(0, 3)
        def _(j):
            cols = pl.ds(pl.multiple_of(j * third, LANES), third)
            y_send[DX_SUM, p, :, cols] = (
                product(dq_s[mine, :], wq[cols, :], 1, 1)
                + product(dk_s[mine, :], wk[cols, :], 1, 1)
                + product(dv_s[mine, :], wv[cols, :], 1, 1)
            ).astype(BF16)

    def weight_grad(m, left, right, first, tile):
        @pl.loop(0, right.shape[1] // tile)
        def _(j):
            cols = pl.ds(pl.multiple_of(j * tile, LANES), tile)
            out_cols = pl.ds(pl.multiple_of(first + j * tile, LANES), tile)
            grad = product(left[...], right[:, cols], 0, 0)
            for r in range(GROUP):
                sb[m, r % 2, (r // 2) % 2, r // 4, :, out_cols] = grad[
                    r * chunk : (r + 1) * chunk, :
                ].astype(BF16)

    def reduce_refs(m):
        if m < 3:
            return sb.at[m], rb0.at[m], rb1.at[m], rb2.at[m]
        return ss, rs0, rs1, rs2

    def core_copy(m):
        mine, r0, _, _ = reduce_refs(m)
        return pltpu.make_async_remote_copy(
            src_ref=mine.at[1 - core],
            dst_ref=r0,
            send_sem=r_ssem.at[m, 0],
            recv_sem=r_rsem.at[m, 0],
            device_id=core_peer,
            device_id_type=MESH,
        )

    def x_copy(m):
        mine, _, r1, _ = reduce_refs(m)
        return pltpu.make_async_remote_copy(
            src_ref=mine.at[core, 1 - xpos],
            dst_ref=r1,
            send_sem=r_ssem.at[m, 1],
            recv_sem=r_rsem.at[m, 1],
            device_id=x_peer,
            device_id_type=MESH,
        )

    def z_copy(m, step):
        mine, _, _, r2 = reduce_refs(m)
        return pltpu.make_async_remote_copy(
            src_ref=mine.at[core, xpos, (zpos + step) % zs],
            dst_ref=r2.at[step - 1],
            send_sem=r_ssem.at[m, 1 + step],
            recv_sem=r_rsem.at[m, 1 + step],
            device_id=z_peer(step),
            device_id_type=MESH,
        )

    def add_into(mine, index, other):
        for zz in range(zs):
            value = mine[(*index, zz)].astype(F32) + other[zz].astype(F32)
            mine[(*index, zz)] = value.astype(mine.dtype)

    def reduce_x(m):
        mine, r0, _, _ = reduce_refs(m)
        core_copy(m).wait_recv()
        add_into(mine, (core, 1 - xpos), r0.at[1 - xpos])
        x_copy(m).start()
        add_into(mine, (core, xpos), r0.at[xpos])

    def reduce_z(m):
        mine, _, r1, _ = reduce_refs(m)
        x_copy(m).wait_recv()
        add_into(mine, (core, xpos), r1)
        for step in range(1, zs):
            z_copy(m, step).start()

    def reduce_end(m):
        mine, _, _, r2 = reduce_refs(m)
        total = mine[core, xpos, zpos].astype(F32)
        for step in range(1, zs):
            z_copy(m, step).wait_recv()
        for step in range(1, zs):
            total = total + r2[step - 1].astype(F32)
        if m < 3:
            grads_out[m] = total
        else:
            small_out[...] = total

    def reduce_sent(m):
        core_copy(m).wait_send()
        x_copy(m).wait_send()
        for step in range(1, zs):
            z_copy(m, step).wait_send()

    def place_vector(row, eight):
        vector = jnp.sum(eight, axis=0, keepdims=True)
        piece = vector.shape[1] // GROUP
        for r in range(GROUP):
            ss[r % 2, (r // 2) % 2, r // 4, row : row + 1, 0:piece] = vector[
                :, r * piece : (r + 1) * piece
            ]

    for p in range(pairs):
        make_inputs(p)
        if p == 0:
            wq_load.wait()
            wk_load.wait()
            wv_load.wait()
        attention(p)
        if p == 0:
            wo_load.wait()
        attention_out(p)
        y_copy(O_SUM, p).start()
    for p in range(pairs):
        y_copy(O_SUM, p).wait_recv()
        norm_one(p)
        if p == 0:
            wi_load.wait()
            w2_load.wait()
        feed_forward(p)
        y_copy(F_SUM, p).start()
    cot_load.wait()
    ss[...] = jnp.zeros(ss.shape, F32)
    for p in range(pairs):
        y_copy(F_SUM, p).wait_recv()
        norm_two(p)
        if p == pairs - 1:
            weight_grad(0, df_s, g_s, 0, FF_TILE)
            core_copy(0).start()
        feed_forward_back(p)
        y_copy(DH_SUM, p).start()
    mixed_copy = pltpu.make_async_copy(out_s, mixed_hbm, out_sem.at[0])
    mixed_copy.start()
    reduce_x(0)
    weight_grad(1, h1_low, du_s, 0, FF_TILE)
    core_copy(1).start()
    place_vector(ROW_G2, acc[A_G2])
    place_vector(ROW_S2, acc[A_S2])
    place_vector(ROW_BOUTER, acc[A_BOUTER])
    place_vector(ROW_BIN, accb[...])
    reduce_x(1)
    for p in range(pairs):
        y_copy(DH_SUM, p).wait_recv()
        norm_one_back(p)
        attention_back(p)
        inputs_back(p)
        y_copy(DX_SUM, p).start()
        if p == 0:
            reduce_z(0)
    weight_grad(2, df_s, att, 0, local)
    weight_grad(2, x_low, dq_s, local, local)
    weight_grad(2, x_low, dk_s, 2 * local, local)
    weight_grad(2, x_low, dv_s, 3 * local, local)
    core_copy(2).start()
    place_vector(ROW_G1, acc[A_G1])
    place_vector(ROW_S1, acc[A_S1])
    place_vector(ROW_BOUT, acc[A_BOUT])
    place_vector(ROW_BQ, accq[0])
    place_vector(ROW_BV, accq[1])
    core_copy(3).start()
    reduce_z(1)
    reduce_x(2)
    reduce_x(3)
    reduce_end(0)
    mixed_copy.wait()

    sums = []
    for p in range(pairs):
        y_copy(DX_SUM, p).wait_recv()

        def step(i, total, p=p):
            size = 32
            here = pl.ds(pl.multiple_of(p * seq + i * size, 16), size)
            dx = dz_s[here, :] + y_sum(DX_SUM, p, i, size)
            out_s[here, :] = dx.astype(BF16)
            return total + jnp.where(i * size >= QLEN, fold_rows(dx), 0.0)

        total = lax.fori_loop(0, seq // 32, step, jnp.zeros((8, width), F32))
        sums.append(jnp.sum(total, axis=0, keepdims=True))
    tgrad_copy = pltpu.make_async_copy(out_s, tgrad_hbm, out_sem.at[1])
    tgrad_copy.start()

    zero_row = jnp.zeros((1, LANES), F32)
    sum_blocks = [
        jnp.concatenate(
            [sums[p][:, j * LANES : (j + 1) * LANES] for j in range(doc_cols)]
            + [zero_row] * (8 - doc_cols),
            axis=0,
        )
        for p in range(pairs)
    ]

    def fill(d, carry):
        for n in range(docs_dev):
            value = jnp.zeros((8, LANES), F32)
            for p in range(pairs):
                value = value + jnp.where(ids[p] == d * docs_dev + n, sum_blocks[p], 0.0)
            doc_part[d, 8 * n : 8 * n + 8, :] = value
        return carry

    lax.fori_loop(0, n_batch, fill, 0)

    def part_copy(step):
        other = (b + step) % n_batch
        return pltpu.make_async_remote_copy(
            src_ref=doc_part.at[other],
            dst_ref=doc_in.at[b],
            send_sem=d_ssem.at[1, step],
            recv_sem=d_rsem.at[1, b],
            device_id=(other, t),
            device_id_type=MESH,
        )

    def part_arrival(step):
        other = (b + step) % n_batch
        return pltpu.make_async_remote_copy(
            src_ref=doc_part.at[other],
            dst_ref=doc_in.at[other],
            send_sem=d_ssem.at[1, step],
            recv_sem=d_rsem.at[1, other],
            device_id=(other, t),
            device_id_type=MESH,
        )

    def part_start(step, carry):
        part_copy(step).start()
        return carry

    def part_wait(step, carry):
        part_arrival(step).wait_recv()
        return carry

    def part_sent(step, carry):
        part_copy(step).wait_send()
        return carry

    lax.fori_loop(1, n_batch, part_start, 0)
    doc_in[b] = doc_part[b]

    reduce_z(2)
    reduce_z(3)
    reduce_end(1)
    lax.fori_loop(1, n_batch, part_wait, 0)

    def add_part(d, total):
        return total + doc_in[d]

    docs_out[...] = lax.fori_loop(0, n_batch, add_part, jnp.zeros(docs_out.shape, F32))
    reduce_end(2)
    reduce_end(3)

    for kind in range(4):
        for p in range(pairs):
            y_copy(kind, p).wait_send()
    for m in range(4):
        reduce_sent(m)
    lax.fori_loop(1, n_batch, doc_sent, 0)
    lax.fori_loop(1, n_batch, part_sent, 0)
    tgrad_copy.wait()


def finish_kernel(
    local, grads_ref, small_ref, docs_ref,
    doc_out, wq_out, bq_out, wk_out, wv_out, bv_out, wo_out, bo_out, g1_out, s1_out,
    wi_out, bi_out, w2_out, b2_out, g2_out, s2_out,
):
    docs_dev, width = doc_out.shape
    for n in range(docs_dev):
        for j in range(width // LANES):
            doc_out[n : n + 1, j * LANES : (j + 1) * LANES] = docs_ref[8 * n + j : 8 * n + j + 1, :]
    w2_out[...] = grads_ref[0]
    wi_out[...] = grads_ref[1]
    wo_out[...] = grads_ref[2, :, 0:local]
    wq_out[...] = grads_ref[2, :, local : 2 * local]
    wk_out[...] = grads_ref[2, :, 2 * local : 3 * local]
    wv_out[...] = grads_ref[2, :, 3 * local : 4 * local]
    for row, out in (
        (ROW_BQ, bq_out), (ROW_BV, bv_out), (ROW_BOUT, bo_out), (ROW_G1, g1_out),
        (ROW_S1, s1_out), (ROW_BIN, bi_out), (ROW_BOUTER, b2_out), (ROW_G2, g2_out),
        (ROW_S2, s2_out),
    ):
        out[...] = small_ref[row, 0 : out.shape[0]]


def body(
    n_batch,
    tokens, doc_vectors, doc_ids, w_query, b_query, w_key, w_value, b_value, w_out, b_out,
    gain_one, shift_one, w_inner, b_inner, w_outer, b_outer, gain_two, shift_two, cotangent,
):
    rows, width = tokens.shape
    pairs = doc_ids.shape[0]
    seq = rows // pairs
    local = w_query.shape[1]
    heads = local // HEAD_DIM
    hidden = w_inner.shape[1]
    docs_dev = doc_vectors.shape[0]
    chunk = width // GROUP
    zs = GROUP // 4
    hbm = pl.BlockSpec(memory_space=pl.ANY)
    vmem = pl.BlockSpec(memory_space=pltpu.VMEM)
    smem = pl.BlockSpec(memory_space=pltpu.SMEM)
    V = pltpu.VMEM
    dma = pltpu.SemaphoreType.DMA
    scratch = [
        V((rows, width), BF16), V((rows, width), BF16),
        V((width, local), BF16), V((width, local), BF16), V((width, local), BF16),
        V((local, width), BF16), V((width, hidden), BF16), V((hidden, width), BF16),
        V((rows, width), BF16),
        V((rows, local), BF16), V((rows, local), BF16), V((rows, local), BF16),
        V((pairs * heads, seq, seq), F32),
        V((rows, local), BF16),
        V((rows, width), F32), V((rows, 1), F32), V((rows, width), BF16),
        V((rows, hidden), BF16), V((rows, hidden), F32),
        V((rows, width), F32), V((rows, width), BF16), V((rows, hidden), BF16),
        V((rows, local), BF16), V((rows, local), BF16), V((rows, local), BF16),
        V((rows, local), BF16),
        V((rows, width), BF16),
        V((6, 8, width), F32), V((8, hidden), F32), V((2, 8, local), F32), V((1, hidden), F32),
        V((4, pairs, seq, width), BF16), V((4, pairs, seq, width), BF16),
        V((3, 2, 2, zs, chunk, hidden), BF16), V((3, 2, zs, chunk, hidden), BF16),
        V((3, zs, chunk, hidden), BF16), V((3, zs - 1, chunk, hidden), BF16),
        V((2, 2, zs, SMALL_ROWS, LANES), F32), V((2, zs, SMALL_ROWS, LANES), F32),
        V((zs, SMALL_ROWS, LANES), F32), V((zs - 1, SMALL_ROWS, LANES), F32),
        V((8 * docs_dev, LANES), BF16), V((n_batch, 8 * docs_dev, LANES), BF16),
        V((n_batch, 8 * docs_dev, LANES), F32), V((n_batch, 8 * docs_dev, LANES), F32),
        dma((4, pairs)), dma((4, pairs)), dma((4, zs + 1)), dma((4, zs + 1)),
        dma((2, n_batch)), dma((2, n_batch)), dma((8,)), dma((2,)),
    ]
    shape = jax.ShapeDtypeStruct
    mixed, tokens_grad, grads, small, docs = pl.pallas_call(
        functools.partial(layer_kernel, (n_batch, pairs, seq)),
        out_shape=(
            shape((rows, width), BF16),
            shape((rows, width), BF16),
            shape((3, chunk, hidden), F32),
            shape((SMALL_ROWS, LANES), F32),
            shape((8 * docs_dev, LANES), F32),
        ),
        in_specs=[hbm] * 8 + [vmem, smem] + [vmem] * 9,
        out_specs=(hbm, hbm, vmem, vmem, vmem),
        scratch_shapes=scratch,
        compiler_params=pltpu.CompilerParams(
            collective_id=0, has_side_effects=True, vmem_limit_bytes=60 * 1024 * 1024
        ),
        name="encoder_layer",
    )(
        tokens, cotangent, w_query, w_key, w_value, w_out, w_inner, w_outer,
        doc_vectors, doc_ids, b_query, b_value, b_out, gain_one, shift_one, b_inner, b_outer,
        gain_two, shift_two,
    )

    inner = n_batch // GROUP
    if inner > 1:
        groups = [[g * inner + i for i in range(inner)] for g in range(GROUP)]
        grads = lax.psum_scatter(
            grads, "batch", scatter_dimension=1, axis_index_groups=groups, tiled=True
        )
        small = lax.psum(small, "batch", axis_index_groups=groups)
        part = lax.axis_index("batch") % inner
        pieces = []
        for row in range(SMALL_ROWS):
            wide = {ROW_BQ: local, ROW_BV: local, ROW_BIN: hidden}.get(row, width)
            size = wide // n_batch
            piece = lax.dynamic_slice(small[row], (part * size,), (size,))
            pieces.append(jnp.pad(piece, (0, LANES - size)))
        small = jnp.stack(pieces)

    out_rows = width // n_batch
    vector = shape((out_rows,), F32)
    vector_local = shape((local // n_batch,), F32)
    square = shape((out_rows, local), F32)
    (
        doc_grad, wq_grad, bq_grad, wk_grad, wv_grad, bv_grad, wo_grad, bo_grad, g1_grad, s1_grad,
        wi_grad, bi_grad, w2_grad, b2_grad, g2_grad, s2_grad,
    ) = pl.pallas_call(
        functools.partial(finish_kernel, local),
        out_shape=(
            shape((docs_dev, width), F32), square, vector_local, square, square, vector_local,
            square, vector, vector, vector,
            shape((out_rows, hidden), F32), shape((hidden // n_batch,), F32),
            shape((out_rows, hidden), F32), vector, vector, vector,
        ),
        in_specs=[vmem] * 3,
        out_specs=(vmem,) * 16,
        name="gradient_outputs",
    )(grads, small, docs)
    return (
        mixed, tokens_grad, doc_grad, wq_grad, bq_grad, wk_grad, wv_grad, bv_grad, wo_grad.T,
        bo_grad, g1_grad, s1_grad, wi_grad, bi_grad, w2_grad.T, b2_grad, g2_grad, s2_grad,
    )


def solution(mesh):
    in_specs = (
        P("batch", None), P("batch", None), P("batch"), P(None, "tensor"), P("tensor"),
        P(None, "tensor"), P(None, "tensor"), P("tensor"), P("tensor", None), P(), P(), P(),
        P(None, "tensor"), P("tensor"), P("tensor", None), P(), P(), P(), P("batch", None),
    )
    out_specs = (
        P("batch", None), P("batch", None), P("batch", None), P("batch", "tensor"),
        P(("tensor", "batch")), P("batch", "tensor"), P("batch", "tensor"),
        P(("tensor", "batch")), P("tensor", "batch"), P("batch"), P("batch"), P("batch"),
        P("batch", "tensor"), P(("tensor", "batch")), P("tensor", "batch"), P("batch"),
        P("batch"), P("batch"),
    )
    return jax.shard_map(
        functools.partial(body, mesh.shape["batch"]),
        mesh=mesh, in_specs=in_specs, out_specs=out_specs, check_vma=False,
    )
```

time: 843 us -> 129 us (0.15)
  waiting for transfers between devices: 578 us -> 0 us
  Pallas kernels: 0 us -> 125 us
  blocking collectives: 84.7 us -> 0 us
  matrix products: 79.5 us -> 0 us
  local copies, waits for them, and re-layouts: 51.1 us -> 3.05 us
  other arithmetic: 23.8 us -> 0 us
  between operations: 17.5 us -> 0.69 us
    reduce_scatter x6 -> x0, waiting for transfers between devices: 395 us -> none  [the longest x1 79.3 us: body(): lax.psum_scatter(grad_w_inner, 'batch', scatter_dimension=0, tiled=True)]
    psum x4 -> x0, waiting for transfers between devices: 182 us -> none  [the longest x1 55.9 us: body(): grad_hidden = grad_sum_two + lax.psum(grad_hidden_part, 'tensor')]
    pallas_call x0 -> x2, Pallas kernels: none -> 125 us  [the longest x1 123 us: body(): pl.pallas_call(functools.partial(layer_kernel, (n_batch, pairs, seq)), ou...]
    dot_general x26 -> x0, matrix products: 79.5 us -> none  [the longest x7 25.2 us: product(): return jnp.dot(left, right, preferred_element_type=jnp.float32)]
    unnamed x1 -> x0, blocking collectives: 61.2 us -> none
    reshape x11 -> x0, local copies, waits for them, and re-layouts: 27.9 us -> none  [the longest x2 5.04 us: body(): grad_attended_heads = grad_attended.astype(jnp.bfloat16).reshape(head_shape)]
    all_gather x1 -> x0, blocking collectives: 23.5 us -> none  [body(): doc_table = lax.all_gather(doc_vectors, 'batch', axis=0, tiled=True)]
    reduce_sum x10 -> x0, other arithmetic: 14.2 us -> none  [the longest x2 4.13 us: normalize(): centre = jnp.mean(summed, axis=-1, keepdims=True)]
  transfers between devices with their start and end apart: 11 -> 0, of which waited for: 10 -> 0; matrix products, arithmetic and copies ran while one was open for 4% -> 0% of each run, Pallas kernels for 0% -> 0%
where the time goes in v1:
time: 129 us
  Pallas kernels  125 us (97%)
  local copies, waits for them, and re-layouts  3.05 us (2%)
    pallas_call x1, Pallas kernels, body(): pl.pallas_call(functools.partial(layer_kernel, (n_batch, pairs, seq)), ou...  123 us
    unnamed x4, local copies, waits for them, and re-layouts  3.05 us

profile of v1, /device:TPU:0, one launch (start us, length us, event | category | flops | bytes accessed | tf_op | source)
XLA Modules:
  0.0 129.0 jit_solution(3605314137392610670)
XLA Ops:
  0.7 123.1 %encoder_layer.1 = (bf16[576,768]{1,0:T(8,128)(2,1)}, bf16[576,768]{1,0:T(8,128)(2,1)}, f32[3,48,1536]{2,1,0:T(8,128)}, f32[16,128]{1,0:T(8,128)}, f32[16,128]{1,0:T(8,128)}) custom-call(bf16[576,768]{1,0:T(8,128)(2,1)} %tokens_hbm.1, bf16[576,768]{1,0:T(8,128)(2,1)} %cot_hbm.1, bf16[768,384]{1,0:T(8,128)(2,1)} %wq_hbm.1, bf16[768,384]{1,0:T(8,128)(2,1)} %wk_hbm.1, ...), custom_call_target="tpu_custom_call" | custom-call | tf_op jit(solution)/shard_map/encoder_layer/pallas_call | solution.py:725
  123.8 0.0 copy-start
  123.8 2.2 %gradient_outputs.1 = (f32[2,768]{1,0:T(2,128)}, f32[48,384]{1,0:T(8,128)}, f32[24]{0:T(128)}, f32[48,384]{1,0:T(8,128)}, f32[48,384]{1,0:T(8,128)}, /*index=5*/...) custom-call(f32[3,48,1536]{2,1,0:T(8,128)} %get-tuple-element.41.gra, ...), custom_call_target="tpu_custom_call" | custom-call | tf_op jit(solution)/shard_map/gradient_outputs/pallas_call | solution.py:770
  126.0 2.1 %copy.39 = bf16[576,768]{1,0:T(8,128)(2,1)} copy(bf16[576,768]{1,0:T(8,128)(2,1)} %get-tuple-element.78) | data formatting | bytes 1769472
  128.1 0.0 copy-done
  128.1 0.9 copy.40
Async XLA Ops:
  123.8 4.4 %copy-start = (bf16[576,768]{1,0:T(8,128)(2,1)S(1)}, bf16[576,768]{1,0:T(8,128)(2,1)}, u32[]{:S(2)}) copy-start(bf16[576,768]{1,0:T(8,128)(2,1)} %get-tuple-element.79) | copy-start | bytes 2654212

commit v2 on v1

v2 whole, which is shorter than its diff:
```python
import functools
import math

import jax
import jax.numpy as jnp
from jax import lax
from jax.experimental import pallas as pl
from jax.experimental.pallas import tpu as pltpu
from jax.sharding import PartitionSpec as P

HEAD_DIM = 64
QLEN = 32
LANES = 128
GROUP = 16
EPSILON = 1e-12
F32 = jnp.float32
BF16 = jnp.bfloat16
MESH = pl.DeviceIdType.MESH

ROW_BQ, ROW_BV, ROW_BOUT, ROW_G1, ROW_S1, ROW_BIN, ROW_BOUTER, ROW_G2, ROW_S2 = range(9)
SMALL_ROWS = 16


def product(left, right, left_dim=1, right_dim=0):
    return lax.dot_general(
        left, right, (((left_dim,), (right_dim,)), ((), ())), preferred_element_type=F32
    )


def fold_rows(block):
    return jnp.sum(block.reshape(block.shape[0] // 8, 8, block.shape[1]), axis=0)


def row_mean(block):
    return jnp.mean(block, axis=1, keepdims=True)


def layer_kernel(
    sizes,
    tokens_hbm, cot_hbm, wq_hbm, wk_hbm, wv_hbm, wo_hbm, wi_hbm, w2_hbm,
    docs_ref, ids_ref, bq_ref, bv_ref, bo_ref, g1_ref, s1_ref, bi_ref, b2_ref, g2_ref, s2_ref,
    mixed_hbm, tgrad_hbm, grads_out, small_out, docs_out,
    tok, cot, w_qkv, wo_all, wi, w2,
    x_low, qkv_s, p_s, att_all, n1_s, r1_s, h1_low, g_s, sl_s, dz_s, df_s, du_s,
    da_s, dqkv_s, out_s, acc, accb, accq, accx,
    y_send, y_recv, ff0, ff1, ff2, ff3, ff4, at0, at1, at2, at3, at4, ss0, ss1, ss2, ss3, ss4,
    doc_stage, doc_table, doc_part, doc_in, sum_send, sum_recv,
    y_ssem, y_rsem, a_ssem, a_rsem, w_ssem, w_rsem, r_ssem, r_rsem, d_ssem, d_rsem,
    s_ssem, s_rsem, load_sem, out_sem,
):
    n_batch, pairs, seq = sizes
    rows, width = tok.shape
    local = wq_hbm.shape[1]
    hidden = wi.shape[1]
    chunk = width // GROUP
    docs_dev = docs_ref.shape[0]
    doc_cols = width // LANES
    inner = n_batch // GROUP

    b = lax.axis_index("batch")
    t = lax.axis_index("tensor")
    place = b // inner
    rest = b % inner
    core = place % 2
    xpos = (place // 2) % 2
    zlow = (place // 4) % 2
    zhigh = place // 8

    def at_place(other):
        return (other * inner + rest, t)

    y_peer = (b, 1 - t)
    core_peer = at_place(place + 1 - 2 * core)
    x_peer = at_place(place + 2 - 4 * xpos)
    zlow_peer = at_place(place + 4 - 8 * zlow)
    zhigh_peer = at_place(place + 8 - 16 * zhigh)

    def batch_peer(step):
        return ((b + step) % n_batch, t)

    wo_mine = pl.ds(pl.multiple_of(t * local, LANES), local)
    att_mine = wo_mine
    loads = []
    for i, (src, dst) in enumerate(
        (
            (tokens_hbm, tok), (wq_hbm, w_qkv.at[:, 0:local]),
            (wk_hbm, w_qkv.at[:, local : 2 * local]), (wv_hbm, w_qkv.at[:, 2 * local :]),
            (wo_hbm, wo_all.at[wo_mine]), (wi_hbm, wi), (w2_hbm, w2), (cot_hbm, cot),
        )
    ):
        copy = pltpu.make_async_copy(src, dst, load_sem.at[i])
        copy.start()
        loads.append(copy)
    (tok_load, wq_load, wk_load, wv_load, wo_load, wi_load, w2_load, cot_load) = loads

    barrier = pltpu.get_barrier_semaphore()

    def greet(step, carry):
        pl.semaphore_signal(barrier, inc=1, device_id=batch_peer(step), device_id_type=MESH)
        return carry

    lax.fori_loop(1, n_batch, greet, 0)
    pl.semaphore_signal(barrier, inc=1, device_id=y_peer, device_id_type=MESH)

    doc_rows = docs_ref[...].astype(F32)
    pieces = []
    for n in range(docs_dev):
        for j in range(8):
            if j < doc_cols:
                pieces.append(doc_rows[n : n + 1, j * LANES : (j + 1) * LANES])
            else:
                pieces.append(jnp.zeros((1, LANES), F32))
    stage = jnp.concatenate(pieces, axis=0).astype(BF16)
    doc_stage[...] = stage
    doc_table[b] = stage

    b_qkv = jnp.concatenate(
        [
            bq_ref[...].astype(F32).reshape(1, local),
            jnp.zeros((1, local), F32),
            bv_ref[...].astype(F32).reshape(1, local),
        ],
        axis=1,
    )
    b_out = bo_ref[...].astype(F32).reshape(1, width)
    gain1 = g1_ref[...].astype(F32).reshape(1, width)
    shift1 = s1_ref[...].astype(F32).reshape(1, width)
    b_inner = bi_ref[...].astype(F32).reshape(1, hidden)
    b_outer = b2_ref[...].astype(F32).reshape(1, width)
    gain2 = g2_ref[...].astype(F32).reshape(1, width)
    shift2 = s2_ref[...].astype(F32).reshape(1, width)

    pl.semaphore_wait(barrier, n_batch)

    share = local // 4

    def share_rows(tensor, first, count):
        start = tensor * local + first * share
        return pl.ds(pl.multiple_of(start, 16), count * share)

    quarter = 2 * core + xpos
    out_weight_copies = [
        pltpu.make_async_remote_copy(
            src_ref=source,
            dst_ref=wo_all.at[target],
            send_sem=w_ssem.at[i],
            recv_sem=w_rsem.at[i],
            device_id=peer,
            device_id_type=MESH,
        )
        for i, (source, target, peer) in enumerate(
            (
                (
                    wo_hbm.at[pl.ds(pl.multiple_of(quarter * share, 16), share)],
                    share_rows(t, quarter, 1),
                    y_peer,
                ),
                (
                    wo_all.at[share_rows(1 - t, quarter, 1)],
                    share_rows(1 - t, quarter, 1),
                    x_peer,
                ),
                (
                    wo_all.at[share_rows(1 - t, 2 * core, 2)],
                    share_rows(1 - t, 2 * core, 2),
                    core_peer,
                ),
            )
        )
    ]
    out_weight_copies[0].start()

    def doc_copy(step):
        return pltpu.make_async_remote_copy(
            src_ref=doc_stage,
            dst_ref=doc_table.at[b],
            send_sem=d_ssem.at[0, step],
            recv_sem=d_rsem.at[0, b],
            device_id=batch_peer(step),
            device_id_type=MESH,
        )

    def doc_arrival(step):
        other = (b + step) % n_batch
        return pltpu.make_async_remote_copy(
            src_ref=doc_stage,
            dst_ref=doc_table.at[other],
            send_sem=d_ssem.at[0, step],
            recv_sem=d_rsem.at[0, other],
            device_id=batch_peer(step),
            device_id_type=MESH,
        )

    def doc_start(step, carry):
        doc_copy(step).start()
        return carry

    def doc_wait(step, carry):
        doc_arrival(step).wait_recv()
        return carry

    def doc_sent(step, carry):
        doc_copy(step).wait_send()
        return carry

    lax.fori_loop(1, n_batch, doc_start, 0)

    tok_load.wait()
    lax.fori_loop(1, n_batch, doc_wait, 0)

    ids = [jnp.full((8, LANES), ids_ref[p], jnp.int32) for p in range(pairs)]

    def pick(d, found):
        block = doc_table[d].astype(F32)
        result = []
        for p in range(pairs):
            value = found[p]
            for n in range(docs_dev):
                value = value + jnp.where(
                    ids[p] == d * docs_dev + n, block[8 * n : 8 * n + 8, :], 0.0
                )
            result.append(value)
        return tuple(result)

    found = lax.fori_loop(
        0, n_batch, pick, tuple(jnp.zeros((8, LANES), F32) for _ in range(pairs))
    )
    doc_row = [
        jnp.concatenate([found[p][j : j + 1, :] for j in range(doc_cols)], axis=1)
        for p in range(pairs)
    ]

    def pair_rows(p):
        return pl.ds(p * seq, seq)

    def inputs_of(p):
        where_row = lax.broadcasted_iota(jnp.int32, (seq, 1), 0)
        return tok[pair_rows(p), :].astype(F32) + jnp.where(where_row >= QLEN, doc_row[p], 0.0)

    half = width // 2

    def half_cols(part):
        return pl.ds(part * half, half)

    def y_copy(kind, p, part):
        return pltpu.make_async_remote_copy(
            src_ref=y_send.at[kind, p, :, half_cols(part)],
            dst_ref=y_recv.at[kind, p, :, half_cols(part)],
            send_sem=y_ssem.at[kind, p, part],
            recv_sem=y_rsem.at[kind, p, part],
            device_id=y_peer,
            device_id_type=MESH,
        )

    def y_wait(kind, p):
        for part in range(2):
            y_copy(kind, p, part).wait_recv()

    def y_sum(kind, p):
        return y_send[kind, p].astype(F32) + y_recv[kind, p].astype(F32)

    F_SUM, DH_SUM, DX_SUM = range(3)

    def att_cols(tensor, j):
        return pl.ds(pl.multiple_of(tensor * local + j * LANES, LANES), LANES)

    def att_copy(p, j):
        place_of = att_all.at[pair_rows(p), att_cols(t, j)]
        return pltpu.make_async_remote_copy(
            src_ref=place_of,
            dst_ref=place_of,
            send_sem=a_ssem.at[p, j],
            recv_sem=a_rsem.at[p, j],
            device_id=y_peer,
            device_id_type=MESH,
        )

    first_lanes = lax.broadcasted_iota(jnp.int32, (1, LANES), 1) < HEAD_DIM

    def head_lanes(values, h):
        keep = first_lanes if h == 0 else jnp.logical_not(first_lanes)
        return jnp.where(keep, values, jnp.zeros_like(values))

    def both_heads(values):
        return jnp.concatenate([head_lanes(values, 0), head_lanes(values, 1)], axis=0)

    def add_acc(which, p, value):
        if p == 0:
            acc[which] = value
        else:
            acc[which] = acc[which] + value

    A_G2, A_S2, A_BOUTER, A_G1, A_S1, A_BOUT = range(6)

    def project(p):
        mine = pair_rows(p)
        x_low[mine, :] = inputs_of(p).astype(BF16)
        qkv_s[mine, :] = (product(x_low[mine, :], w_qkv[...]) + b_qkv).astype(BF16)

    def qkv(kind, j):
        return pl.ds(kind * local + j * LANES, LANES)

    def attention(p):
        mine = pair_rows(p)
        for j in range(local // LANES):
            kk, vv = qkv_s[mine, qkv(1, j)], qkv_s[mine, qkv(2, j)]
            qq = (qkv_s[mine, qkv(0, j)].astype(F32) * 0.125).astype(BF16)
            qkv_s[mine, qkv(0, j)] = qq
            low = []
            for h in range(2):
                scores = product(head_lanes(qq, h), kk, 1, 1)
                expo = jnp.exp(scores - jnp.max(scores, axis=1, keepdims=True))
                probs = expo * (1.0 / jnp.sum(expo, axis=1, keepdims=True))
                p_s[p * (local // HEAD_DIM) + 2 * j + h] = probs
                low.append(probs.astype(BF16))
            both = product(low[0], head_lanes(vv, 0)) + product(low[1], head_lanes(vv, 1))
            att_all[mine, att_cols(t, j)] = both.astype(BF16)
            att_copy(p, j).start()

    def attention_out(p):
        for j in range(local // LANES):
            att_copy(p, j).wait_recv()
        mine = pair_rows(p)
        summed = inputs_of(p) + (product(att_all[mine, :], wo_all[...]) + b_out)
        centered = summed - row_mean(summed)
        inverse = lax.rsqrt(row_mean(centered * centered) + EPSILON)
        normed = centered * inverse
        n1_s[mine, :] = normed
        r1_s[mine, :] = inverse
        h1_low[mine, :] = (normed * gain1 + shift1).astype(BF16)

    FF_TILE = 512

    def feed_forward(p):
        mine = pair_rows(p)
        u = product(h1_low[mine, :], wi[...]) + b_inner
        cdf = 0.5 * (1.0 + lax.erf(u * (1.0 / math.sqrt(2.0))))
        density = jnp.exp(-0.5 * u * u) * (1.0 / math.sqrt(2.0 * math.pi))
        g_s[mine, :] = (u * cdf).astype(BF16)
        sl_s[mine, :] = cdf + u * density
        for part in range(2):
            cols = half_cols(part)
            y_send[F_SUM, p, :, cols] = product(g_s[mine, :], w2[:, cols]).astype(BF16)
            y_copy(F_SUM, p, part).start()

    def norm_two(p):
        mine = pair_rows(p)
        h1 = n1_s[mine, :] * gain1 + shift1
        summed = h1 + (y_sum(F_SUM, p) + b_outer)
        centered = summed - row_mean(summed)
        inverse = lax.rsqrt(row_mean(centered * centered) + EPSILON)
        normed = centered * inverse
        out_s[mine, :] = (normed * gain2 + shift2).astype(BF16)
        dy = cot[mine, :].astype(F32)
        scaled = dy * gain2
        dz = inverse * (scaled - row_mean(scaled) - normed * row_mean(scaled * normed))
        dz_s[mine, :] = dz
        df_s[mine, :] = dz.astype(BF16)
        add_acc(A_G2, p, fold_rows(dy * normed))
        add_acc(A_S2, p, fold_rows(dy))
        add_acc(A_BOUTER, p, fold_rows(dz))

    def feed_forward_back(p):
        mine = pair_rows(p)
        du = (product(df_s[mine, :], w2[...], 1, 1) * sl_s[mine, :]).astype(BF16)
        du_s[mine, :] = du
        total = fold_rows(du.astype(F32))
        if p == 0:
            accb[...] = total
        else:
            accb[...] = accb[...] + total
        for part in range(2):
            cols = half_cols(part)
            y_send[DH_SUM, p, :, cols] = product(du_s[mine, :], wi[cols, :], 1, 1).astype(BF16)
            y_copy(DH_SUM, p, part).start()

    def norm_one_back(p):
        mine = pair_rows(p)
        dh = dz_s[mine, :] + y_sum(DH_SUM, p)
        normed = n1_s[mine, :]
        scaled = dh * gain1
        dz = r1_s[mine, :] * (scaled - row_mean(scaled) - normed * row_mean(scaled * normed))
        dz_s[mine, :] = dz
        df_s[mine, :] = dz.astype(BF16)
        doc_part_rows = fold_rows(dz[QLEN:, :])
        accx[p] = doc_part_rows
        add_acc(A_G1, p, fold_rows(dh * normed))
        add_acc(A_S1, p, fold_rows(dh))
        add_acc(A_BOUT, p, doc_part_rows + fold_rows(dz[:QLEN, :]))

    def attention_back(p):
        mine = pair_rows(p)
        da_s[mine, :] = product(df_s[mine, :], wo_all[wo_mine, :], 1, 1).astype(BF16)
        for j in range(local // LANES):
            qq, kk, vv = (qkv_s[mine, qkv(kind, j)] for kind in range(3))
            dd = da_s[mine, pl.ds(j * LANES, LANES)]
            low, ds = [], []
            for h in range(2):
                probs = p_s[p * (local // HEAD_DIM) + 2 * j + h]
                low.append(probs.astype(BF16))
                dp = product(head_lanes(dd, h), vv, 1, 1)
                slope = probs * (dp - jnp.sum(probs * dp, axis=1, keepdims=True))
                ds.append(slope.astype(BF16))
            dv = product(jnp.concatenate(low, axis=0), both_heads(dd), 0, 0)
            dk = product(jnp.concatenate(ds, axis=0), both_heads(qq), 0, 0)
            dq = product(ds[0], head_lanes(kk, 0)) + product(ds[1], head_lanes(kk, 1))
            dqkv_s[mine, qkv(0, j)] = (dq * 0.125).astype(BF16)
            dqkv_s[mine, qkv(1, j)] = dk.astype(BF16)
            dqkv_s[mine, qkv(2, j)] = dv.astype(BF16)
        for i, kind in enumerate((0, 2)):
            total = fold_rows(dqkv_s[mine, pl.ds(kind * local, local)].astype(F32))
            if p == 0:
                accq[i] = total
            else:
                accq[i] = accq[i] + total

    def inputs_back(p):
        mine = pair_rows(p)
        part = product(dqkv_s[mine, :], w_qkv[...], 1, 1)
        y_send[DX_SUM, p] = part.astype(BF16)
        accx[p] = jnp.where(t == 0, accx[p], 0.0) + fold_rows(part[QLEN:, :])

    def inputs_send(p):
        for part in range(2):
            y_copy(DX_SUM, p, part).start()

    N_FF = 6
    N_PIECES = 11
    Z_FIRST = (1, 2, 4)

    def piece_refs(m):
        if m < N_FF:
            return [ref.at[m] for ref in (ff0, ff1, ff2, ff3, ff4)]
        if m < N_PIECES - 1:
            return [ref.at[m - N_FF] for ref in (at0, at1, at2, at3, at4)]
        return [ss0, ss1, ss2, ss3, ss4]

    def chunk_index(m, r):
        low, mid, high, top = r % 2, (r // 2) % 2, (r // 4) % 2, r // 8
        return (low, high, mid, top) if m in Z_FIRST else (low, mid, high, top)

    def my_index(m):
        return (core, zlow, xpos, zhigh) if m in Z_FIRST else (core, xpos, zlow, zhigh)

    def piece_copy(m, phase):
        refs = piece_refs(m)
        index = my_index(m)
        peers = (core_peer, x_peer, zlow_peer, zhigh_peer)
        if m in Z_FIRST:
            peers = (core_peer, zlow_peer, x_peer, zhigh_peer)
        return pltpu.make_async_remote_copy(
            src_ref=refs[0].at[(*index[:phase], 1 - index[phase])],
            dst_ref=refs[phase + 1],
            send_sem=r_ssem.at[m, phase],
            recv_sem=r_rsem.at[m, phase],
            device_id=peers[phase],
            device_id_type=MESH,
        )

    def add_piece(mine, index, other, lead):
        if lead == 0:
            value = mine[index].astype(F32) + other[...].astype(F32)
            mine[index] = value.astype(mine.dtype)
            return
        for k in range(2):
            add_piece(mine, (*index, k), other.at[k], lead - 1)

    def advance(m, phase):
        refs = piece_refs(m)
        index = my_index(m)
        piece_copy(m, phase - 1).wait_recv()
        mine, other = refs[0], refs[phase]
        away, stay = 1 - index[phase], index[phase]
        add_piece(mine, (*index[:phase], away), other.at[away], 3 - phase)
        piece_copy(m, phase).start()
        add_piece(mine, (*index[:phase], stay), other.at[stay], 3 - phase)

    def complete(m):
        refs = piece_refs(m)
        index = my_index(m)
        piece_copy(m, 3).wait_recv()
        total = refs[0][index].astype(F32) + refs[4][...].astype(F32)
        if m < N_FF:
            grads_out[m // 3, :, (m % 3) * FF_TILE : (m % 3 + 1) * FF_TILE] = total
        elif m < N_PIECES - 1:
            n = m - N_FF
            grads_out[2, :, n * local : (n + 1) * local] = total
        else:
            small_out[...] = total

    def weight_grad(m, left, right):
        refs = piece_refs(m)
        grad = product(left, right, 0, 0)
        for r in range(GROUP):
            refs[0][chunk_index(m, r)] = grad[r * chunk : (r + 1) * chunk, :].astype(BF16)
        piece_copy(m, 0).start()

    def outer_grad(n):
        weight_grad(n, df_s[...], g_s[:, n * FF_TILE : (n + 1) * FF_TILE])

    def inner_grad(n):
        weight_grad(3 + n, h1_low[...], du_s[:, n * FF_TILE : (n + 1) * FF_TILE])

    def place_vector(row, eight):
        vector = jnp.sum(eight, axis=0, keepdims=True)
        piece = vector.shape[1] // GROUP
        for r in range(GROUP):
            ss0[(*chunk_index(SMALL, r), slice(row, row + 1), slice(0, piece))] = vector[
                :, r * piece : (r + 1) * piece
            ]

    OUT, QUERY, KEY, VALUE, SMALL = range(N_FF, N_PIECES)

    def qkv_grad(m):
        kind = m - QUERY
        weight_grad(m, x_low[...], dqkv_s[:, kind * local : (kind + 1) * local])

    zero_row = jnp.zeros((1, LANES), F32)
    sum_copy = pltpu.make_async_remote_copy(
        src_ref=sum_send,
        dst_ref=sum_recv,
        send_sem=s_ssem.at[0],
        recv_sem=s_rsem.at[0],
        device_id=y_peer,
        device_id_type=MESH,
    )

    def send_document_sums():
        for p in range(pairs):
            row = jnp.sum(accx[p], axis=0, keepdims=True)
            sum_send[p] = jnp.concatenate(
                [row[:, j * LANES : (j + 1) * LANES] for j in range(doc_cols)]
                + [zero_row] * (8 - doc_cols),
                axis=0,
            )
        sum_copy.start()

    def part_copy(step):
        other = (b + step) % n_batch
        return pltpu.make_async_remote_copy(
            src_ref=doc_part.at[other],
            dst_ref=doc_in.at[b],
            send_sem=d_ssem.at[1, step],
            recv_sem=d_rsem.at[1, b],
            device_id=(other, t),
            device_id_type=MESH,
        )

    def part_arrival(step):
        other = (b + step) % n_batch
        return pltpu.make_async_remote_copy(
            src_ref=doc_part.at[other],
            dst_ref=doc_in.at[other],
            send_sem=d_ssem.at[1, step],
            recv_sem=d_rsem.at[1, other],
            device_id=(other, t),
            device_id_type=MESH,
        )

    def part_start(step, carry):
        part_copy(step).start()
        return carry

    def part_wait(step, carry):
        part_arrival(step).wait_recv()
        return carry

    def part_sent(step, carry):
        part_copy(step).wait_send()
        return carry

    def send_document_parts():
        sum_copy.wait_recv()
        sum_blocks = [sum_send[p] + sum_recv[p] for p in range(pairs)]

        def fill(d, carry):
            for n in range(docs_dev):
                value = jnp.zeros((8, LANES), F32)
                for p in range(pairs):
                    value = value + jnp.where(ids[p] == d * docs_dev + n, sum_blocks[p], 0.0)
                doc_part[d, 8 * n : 8 * n + 8, :] = value
            return carry

        lax.fori_loop(0, n_batch, fill, 0)
        lax.fori_loop(1, n_batch, part_start, 0)
        doc_in[b] = doc_part[b]

    def add_document_parts():
        lax.fori_loop(1, n_batch, part_wait, 0)

        def add_part(d, total):
            return total + doc_in[d]

        docs_out[...] = lax.fori_loop(0, n_batch, add_part, jnp.zeros(docs_out.shape, F32))

    def input_grad(p):
        y_wait(DX_SUM, p)
        out_s[pair_rows(p), :] = (dz_s[pair_rows(p), :] + y_sum(DX_SUM, p)).astype(BF16)
        copy = pltpu.make_async_copy(
            out_s.at[pair_rows(p)], tgrad_hbm.at[pair_rows(p)], out_sem.at[1 + p]
        )
        copy.start()
        return copy

    wq_load.wait()
    wk_load.wait()
    wv_load.wait()
    project(0)
    out_weight_copies[0].wait_recv()
    out_weight_copies[1].start()
    attention(0)
    project(1)
    attention(1)
    out_weight_copies[1].wait_recv()
    out_weight_copies[2].start()
    wo_load.wait()
    out_weight_copies[2].wait_recv()
    wi_load.wait()
    w2_load.wait()
    attention_out(0)
    feed_forward(0)
    attention_out(1)
    feed_forward(1)
    cot_load.wait()
    y_wait(F_SUM, 0)
    norm_two(0)
    feed_forward_back(0)
    y_wait(F_SUM, 1)
    norm_two(1)
    mixed_copy = pltpu.make_async_copy(out_s, mixed_hbm, out_sem.at[0])
    mixed_copy.start()
    outer_grad(1)
    outer_grad(0)
    feed_forward_back(1)
    advance(1, 1)
    inner_grad(1)
    advance(0, 1)
    outer_grad(2)
    inner_grad(2)
    ss0[...] = jnp.zeros(ss0.shape, F32)
    place_vector(ROW_G2, acc[A_G2])
    place_vector(ROW_S2, acc[A_S2])
    place_vector(ROW_BOUTER, acc[A_BOUTER])
    place_vector(ROW_BIN, accb[...])
    inner_grad(0)
    advance(2, 1)
    advance(4, 1)
    advance(5, 1)
    y_wait(DH_SUM, 0)
    norm_one_back(0)
    attention_back(0)
    inputs_back(0)
    inputs_send(0)
    advance(1, 2)
    advance(0, 2)
    advance(3, 1)
    advance(2, 2)
    advance(5, 2)
    advance(1, 3)
    advance(4, 2)
    y_wait(DH_SUM, 1)
    norm_one_back(1)
    weight_grad(OUT, df_s[...], att_all[:, att_mine])
    attention_back(1)
    advance(5, 3)
    qkv_grad(KEY)
    qkv_grad(VALUE)
    advance(OUT, 1)
    complete(1)
    advance(0, 3)
    inputs_back(1)
    send_document_sums()
    inputs_send(1)
    mixed_copy.wait()
    advance(KEY, 1)
    advance(4, 3)
    advance(3, 2)
    complete(5)
    advance(VALUE, 1)
    qkv_grad(QUERY)
    advance(2, 3)
    tgrad_copies = [input_grad(0)]
    place_vector(ROW_G1, acc[A_G1])
    place_vector(ROW_S1, acc[A_S1])
    place_vector(ROW_BOUT, acc[A_BOUT])
    place_vector(ROW_BQ, accq[0])
    place_vector(ROW_BV, accq[1])
    piece_copy(SMALL, 0).start()
    complete(0)
    send_document_parts()
    advance(OUT, 2)
    advance(QUERY, 1)
    advance(SMALL, 1)
    complete(4)
    advance(3, 3)
    advance(KEY, 2)
    add_document_parts()
    complete(2)
    advance(OUT, 3)
    advance(VALUE, 2)
    complete(3)
    advance(KEY, 3)
    tgrad_copies.append(input_grad(1))
    advance(QUERY, 2)
    complete(OUT)
    advance(VALUE, 3)
    advance(SMALL, 2)
    complete(KEY)
    advance(QUERY, 3)
    advance(SMALL, 3)
    complete(VALUE)
    complete(QUERY)
    complete(SMALL)
    for copy in out_weight_copies:
        copy.wait_send()
    sum_copy.wait_send()
    for p in range(pairs):
        for j in range(local // LANES):
            att_copy(p, j).wait_send()
        for kind in range(3):
            for part in range(2):
                y_copy(kind, p, part).wait_send()
    for m in range(N_PIECES):
        for phase in range(4):
            piece_copy(m, phase).wait_send()
    lax.fori_loop(1, n_batch, doc_sent, 0)
    lax.fori_loop(1, n_batch, part_sent, 0)
    for copy in tgrad_copies:
        copy.wait()


def finish_kernel(
    local, mixed_ref, tgrad_ref, grads_ref, small_ref, docs_ref,
    mixed_out, tgrad_out, doc_out, wq_out, bq_out, wk_out, wv_out, bv_out, wo_out, bo_out,
    g1_out, s1_out, wi_out, bi_out, w2_out, b2_out, g2_out, s2_out,
    rows_held, grads_held, in_sem, out_sem,
):
    half = mixed_ref.shape[0] // 2
    moves = []
    for i, (source, target) in enumerate(((mixed_ref, mixed_out), (tgrad_ref, tgrad_out))):
        for k in range(2):
            part = pl.ds(k * half, half)
            moves.append((source.at[part], rows_held.at[i, part], [(rows_held.at[i, part], target.at[part])]))
    for m, targets in enumerate(((w2_out,), (wi_out,), (wo_out, wq_out, wk_out, wv_out))):
        stores = [
            (grads_held.at[m, :, pl.ds(n * local, local)] if m == 2 else grads_held.at[m], target)
            for n, target in enumerate(targets)
        ]
        moves.append((grads_ref.at[m], grads_held.at[m], stores))
    loads = [
        pltpu.make_async_copy(source, held, in_sem.at[i])
        for i, (source, held, _) in enumerate(moves)
    ]
    for copy in loads:
        copy.start()
    docs_dev, width = doc_out.shape
    for n in range(docs_dev):
        for j in range(width // LANES):
            doc_out[n : n + 1, j * LANES : (j + 1) * LANES] = docs_ref[8 * n + j : 8 * n + j + 1, :]
    for row, out in (
        (ROW_BQ, bq_out), (ROW_BV, bv_out), (ROW_BOUT, bo_out), (ROW_G1, g1_out),
        (ROW_S1, s1_out), (ROW_BIN, bi_out), (ROW_BOUTER, b2_out), (ROW_G2, g2_out),
        (ROW_S2, s2_out),
    ):
        out[...] = small_ref[row, 0 : out.shape[0]]
    stored = []
    for copy, (_, _, stores) in zip(loads, moves):
        copy.wait()
        for source, target in stores:
            stored.append(pltpu.make_async_copy(source, target, out_sem.at[len(stored)]))
            stored[-1].start()
    for copy in stored:
        copy.wait()


def body(
    n_batch,
    tokens, doc_vectors, doc_ids, w_query, b_query, w_key, w_value, b_value, w_out, b_out,
    gain_one, shift_one, w_inner, b_inner, w_outer, b_outer, gain_two, shift_two, cotangent,
):
    rows, width = tokens.shape
    pairs = doc_ids.shape[0]
    seq = rows // pairs
    local = w_query.shape[1]
    heads = local // HEAD_DIM
    hidden = w_inner.shape[1]
    docs_dev = doc_vectors.shape[0]
    chunk = width // GROUP
    part = hidden // 3
    hbm = pl.BlockSpec(memory_space=pl.ANY)
    vmem = pl.BlockSpec(memory_space=pltpu.VMEM)
    smem = pl.BlockSpec(memory_space=pltpu.SMEM)
    V = pltpu.VMEM
    dma = pltpu.SemaphoreType.DMA
    scratch = [
        V((rows, width), BF16), V((rows, width), BF16),
        V((width, 3 * local), BF16), V((width, width), BF16), V((width, hidden), BF16), V((hidden, width), BF16),
        V((rows, width), BF16),
        V((rows, 3 * local), BF16),
        V((pairs * heads, seq, seq), F32),
        V((rows, width), BF16),
        V((rows, width), F32), V((rows, 1), F32), V((rows, width), BF16),
        V((rows, hidden), BF16), V((rows, hidden), F32),
        V((rows, width), F32), V((rows, width), BF16), V((rows, hidden), BF16),
        V((rows, local), BF16), V((rows, 3 * local), BF16),
        V((rows, width), BF16),
        V((6, 8, width), F32), V((8, hidden), F32), V((2, 8, local), F32),
        V((pairs, 8, width), F32),
        V((3, pairs, seq, width), BF16), V((3, pairs, seq, width), BF16),
        *[V((6, *(2,) * n, chunk, part), BF16) for n in (4, 3, 2, 1, 0)],
        *[V((4, *(2,) * n, chunk, local), BF16) for n in (4, 3, 2, 1, 0)],
        *[V((*(2,) * n, SMALL_ROWS, LANES), F32) for n in (4, 3, 2, 1, 0)],
        V((8 * docs_dev, LANES), BF16), V((n_batch, 8 * docs_dev, LANES), BF16),
        V((n_batch, 8 * docs_dev, LANES), F32), V((n_batch, 8 * docs_dev, LANES), F32),
        V((pairs, 8, LANES), F32), V((pairs, 8, LANES), F32),
        dma((3, pairs, 2)), dma((3, pairs, 2)), dma((pairs, local // LANES)),
        dma((pairs, local // LANES)), dma((3,)), dma((3,)), dma((11, 4)), dma((11, 4)),
        dma((2, n_batch)), dma((2, n_batch)), dma((1,)), dma((1,)), dma((8,)), dma((1 + pairs,)),
    ]
    shape = jax.ShapeDtypeStruct
    mixed, tokens_grad, grads, small, docs = pl.pallas_call(
        functools.partial(layer_kernel, (n_batch, pairs, seq)),
        out_shape=(
            shape((rows, width), BF16),
            shape((rows, width), BF16),
            shape((3, chunk, hidden), F32),
            shape((SMALL_ROWS, LANES), F32),
            shape((8 * docs_dev, LANES), F32),
        ),
        in_specs=[hbm] * 8 + [vmem, smem] + [vmem] * 9,
        out_specs=(hbm, hbm, vmem, vmem, vmem),
        scratch_shapes=scratch,
        compiler_params=pltpu.CompilerParams(
            collective_id=0, has_side_effects=True, vmem_limit_bytes=60 * 1024 * 1024
        ),
        name="encoder_layer",
    )(
        tokens, cotangent, w_query, w_key, w_value, w_out, w_inner, w_outer,
        doc_vectors, doc_ids, b_query, b_value, b_out, gain_one, shift_one, b_inner, b_outer,
        gain_two, shift_two,
    )

    inner = n_batch // GROUP
    if inner > 1:
        groups = [[g * inner + i for i in range(inner)] for g in range(GROUP)]
        grads = lax.psum_scatter(
            grads, "batch", scatter_dimension=1, axis_index_groups=groups, tiled=True
        )
        small = lax.psum(small, "batch", axis_index_groups=groups)
        part = lax.axis_index("batch") % inner
        pieces = []
        for row in range(SMALL_ROWS):
            wide = {ROW_BQ: local, ROW_BV: local, ROW_BIN: hidden}.get(row, width)
            size = wide // n_batch
            piece = lax.dynamic_slice(small[row], (part * size,), (size,))
            pieces.append(jnp.pad(piece, (0, LANES - size)))
        small = jnp.stack(pieces)

    out_rows = width // n_batch
    vector = shape((out_rows,), F32)
    vector_local = shape((local // n_batch,), F32)
    square = shape((out_rows, local), F32)
    (
        mixed, tokens_grad, doc_grad, wq_grad, bq_grad, wk_grad, wv_grad, bv_grad, wo_grad, bo_grad, g1_grad, s1_grad,
        wi_grad, bi_grad, w2_grad, b2_grad, g2_grad, s2_grad,
    ) = pl.pallas_call(
        functools.partial(finish_kernel, local),
        out_shape=(
            shape((rows, width), BF16), shape((rows, width), BF16),
            shape((docs_dev, width), F32), square, vector_local, square, square, vector_local,
            square, vector, vector, vector,
            shape((out_rows, hidden), F32), shape((hidden // n_batch,), F32),
            shape((out_rows, hidden), F32), vector, vector, vector,
        ),
        in_specs=[hbm, hbm, hbm, vmem, vmem],
        out_specs=(
            hbm, hbm, vmem, hbm, vmem, hbm, hbm, vmem, hbm, vmem, vmem, vmem, hbm, vmem, hbm,
            vmem, vmem, vmem,
        ),
        scratch_shapes=[
            V((2, rows, width), BF16), V((3, out_rows, hidden), F32), dma((7,)), dma((10,)),
        ],
        name="gradient_outputs",
    )(mixed, tokens_grad, grads, small, docs)
    return (
        mixed, tokens_grad, doc_grad, wq_grad, bq_grad, wk_grad, wv_grad, bv_grad, wo_grad.T,
        bo_grad, g1_grad, s1_grad, wi_grad, bi_grad, w2_grad.T, b2_grad, g2_grad, s2_grad,
    )


def solution(mesh):
    in_specs = (
        P("batch", None), P("batch", None), P("batch"), P(None, "tensor"), P("tensor"),
        P(None, "tensor"), P(None, "tensor"), P("tensor"), P("tensor", None), P(), P(), P(),
        P(None, "tensor"), P("tensor"), P("tensor", None), P(), P(), P(), P("batch", None),
    )
    out_specs = (
        P("batch", None), P("batch", None), P("batch", None), P("batch", "tensor"),
        P(("tensor", "batch")), P("batch", "tensor"), P("batch", "tensor"),
        P(("tensor", "batch")), P("tensor", "batch"), P("batch"), P("batch"), P("batch"),
        P("batch", "tensor"), P(("tensor", "batch")), P("tensor", "batch"), P("batch"),
        P("batch"), P("batch"),
    )
    return jax.shard_map(
        functools.partial(body, mesh.shape["batch"]),
        mesh=mesh, in_specs=in_specs, out_specs=out_specs, check_vma=False,
    )
```

time: 129 us -> 103 us (0.80)
  Pallas kernels: 125 us -> 102 us
  local copies, waits for them, and re-layouts: 3.05 us -> 0 us
    pallas_call x1, Pallas kernels: 123 us -> 98.2 us  [body(): pl.pallas_call(functools.partial(layer_kernel, (n_batch, pairs, seq)), ou...]
    unnamed x4 -> x0, local copies, waits for them, and re-layouts: 3.05 us -> none
    pallas_call x1, Pallas kernels: 2.22 us -> 3.99 us  [body(): pl.pallas_call(functools.partial(finish_kernel, local), out_shape=(shape(...]
where the time goes in v2:
time: 103 us
  Pallas kernels  102 us (99%)
    pallas_call x1, Pallas kernels, body(): pl.pallas_call(functools.partial(layer_kernel, (n_batch, pairs, seq)), ou...  98.2 us
    pallas_call x1, Pallas kernels, body(): pl.pallas_call(functools.partial(finish_kernel, local), out_shape=(shape(...  3.99 us

profile of v2, /device:TPU:0, one launch (start us, length us, event | category | flops | bytes accessed | tf_op | source)
XLA Modules:
  0.0 103.0 jit_solution(13234195212069774662)
XLA Ops:
  0.7 98.2 %encoder_layer.1 = (bf16[576,768]{1,0:T(8,128)(2,1)}, bf16[576,768]{1,0:T(8,128)(2,1)}, f32[3,48,1536]{2,1,0:T(8,128)}, f32[16,128]{1,0:T(8,128)}, f32[16,128]{1,0:T(8,128)}) custom-call(bf16[576,768]{1,0:T(8,128)(2,1)} %tokens_hbm.1, bf16[576,768]{1,0:T(8,128)(2,1)} %cot_hbm.1, bf16[768,384]{1,0:T(8,128)(2,1)} %wq_hbm.1, bf16[768,384]{1,0:T(8,128)(2,1)} %wk_hbm.1, ...), custom_call_target="tpu_custom_call" | custom-call | tf_op jit(solution)/shard_map/encoder_layer/pallas_call | solution.py:821
  98.8 4.0 %gradient_outputs.1 = (bf16[576,768]{1,0:T(8,128)(2,1)}, bf16[576,768]{1,0:T(8,128)(2,1)}, f32[2,768]{1,0:T(2,128)}, f32[48,384]{1,0:T(8,128)}, f32[24]{0:T(128)...) custom-call(bf16[576,768]{1,0:T(8,128)(2,1)} %get-tuple-element.41.m, ...), custom_call_target="tpu_custom_call" | custom-call | tf_op jit(solution)/shard_map/gradient_outputs/pallas_call | solution.py:866

commit v3 on v2

--- a/solution.py
+++ b/solution.py
@@ -39,14 +39,14 @@
     sizes,
     tokens_hbm, cot_hbm, wq_hbm, wk_hbm, wv_hbm, wo_hbm, wi_hbm, w2_hbm,
     docs_ref, ids_ref, bq_ref, bv_ref, bo_ref, g1_ref, s1_ref, bi_ref, b2_ref, g2_ref, s2_ref,
-    mixed_hbm, tgrad_hbm, grads_out, small_out, docs_out,
+    mixed_out, tgrad_out, grads_out, small_out, docs_out,
     tok, cot, w_qkv, wo_all, wi, w2,
     x_low, qkv_s, p_s, att_all, n1_s, r1_s, h1_low, g_s, sl_s, dz_s, df_s, du_s,
-    da_s, dqkv_s, out_s, acc, accb, accq, accx,
+    da_s, dqkv_s, acc, accb, accq, accx,
     y_send, y_recv, ff0, ff1, ff2, ff3, ff4, at0, at1, at2, at3, at4, ss0, ss1, ss2, ss3, ss4,
     doc_stage, doc_table, doc_part, doc_in, sum_send, sum_recv,
     y_ssem, y_rsem, a_ssem, a_rsem, w_ssem, w_rsem, r_ssem, r_rsem, d_ssem, d_rsem,
-    s_ssem, s_rsem, load_sem, out_sem,
+    s_ssem, s_rsem, load_sem,
 ):
     n_batch, pairs, seq = sizes
     rows, width = tok.shape
@@ -78,6 +78,15 @@
     def batch_peer(step):
         return ((b + step) % n_batch, t)
 
+    barrier = pltpu.get_barrier_semaphore()
+
+    def greet(step, carry):
+        pl.semaphore_signal(barrier, inc=1, device_id=batch_peer(step), device_id_type=MESH)
+        return carry
+
+    lax.fori_loop(1, n_batch, greet, 0)
+    pl.semaphore_signal(barrier, inc=1, device_id=y_peer, device_id_type=MESH)
+
     wo_mine = pl.ds(pl.multiple_of(t * local, LANES), local)
     att_mine = wo_mine
     loads = []
@@ -92,15 +101,6 @@
         copy.start()
         loads.append(copy)
     (tok_load, wq_load, wk_load, wv_load, wo_load, wi_load, w2_load, cot_load) = loads
-
-    barrier = pltpu.get_barrier_semaphore()
-
-    def greet(step, carry):
-        pl.semaphore_signal(barrier, inc=1, device_id=batch_peer(step), device_id_type=MESH)
-        return carry
-
-    lax.fori_loop(1, n_batch, greet, 0)
-    pl.semaphore_signal(barrier, inc=1, device_id=y_peer, device_id_type=MESH)
 
     doc_rows = docs_ref[...].astype(F32)
     pieces = []
@@ -350,7 +350,7 @@
         centered = summed - row_mean(summed)
         inverse = lax.rsqrt(row_mean(centered * centered) + EPSILON)
         normed = centered * inverse
-        out_s[mine, :] = (normed * gain2 + shift2).astype(BF16)
+        mixed_out[mine, :] = (normed * gain2 + shift2).astype(BF16)
         dy = cot[mine, :].astype(F32)
         scaled = dy * gain2
         dz = inverse * (scaled - row_mean(scaled) - normed * row_mean(scaled * normed))
@@ -426,7 +426,8 @@
 
     N_FF = 6
     N_PIECES = 11
-    Z_FIRST = (1, 2, 4)
+    X_Z, Z_X_Z, Z_Z_X = (0, 1, 2, 3), (0, 2, 1, 3), (0, 2, 3, 1)
+    HALVING = (Z_Z_X, X_Z, Z_Z_X, X_Z, X_Z, X_Z, X_Z, X_Z, X_Z, Z_X_Z, X_Z)
 
     def piece_refs(m):
         if m < N_FF:
@@ -436,24 +437,22 @@
         return [ss0, ss1, ss2, ss3, ss4]
 
     def chunk_index(m, r):
-        low, mid, high, top = r % 2, (r // 2) % 2, (r // 4) % 2, r // 8
-        return (low, high, mid, top) if m in Z_FIRST else (low, mid, high, top)
+        bits = (r % 2, (r // 2) % 2, (r // 4) % 2, r // 8)
+        return tuple(bits[k] for k in HALVING[m])
 
     def my_index(m):
-        return (core, zlow, xpos, zhigh) if m in Z_FIRST else (core, xpos, zlow, zhigh)
+        return tuple((core, xpos, zlow, zhigh)[k] for k in HALVING[m])
 
     def piece_copy(m, phase):
         refs = piece_refs(m)
         index = my_index(m)
         peers = (core_peer, x_peer, zlow_peer, zhigh_peer)
-        if m in Z_FIRST:
-            peers = (core_peer, zlow_peer, x_peer, zhigh_peer)
         return pltpu.make_async_remote_copy(
             src_ref=refs[0].at[(*index[:phase], 1 - index[phase])],
             dst_ref=refs[phase + 1],
             send_sem=r_ssem.at[m, phase],
             recv_sem=r_rsem.at[m, phase],
-            device_id=peers[phase],
+            device_id=peers[HALVING[m][phase]],
             device_id_type=MESH,
         )
 
@@ -595,12 +594,7 @@
 
     def input_grad(p):
         y_wait(DX_SUM, p)
-        out_s[pair_rows(p), :] = (dz_s[pair_rows(p), :] + y_sum(DX_SUM, p)).astype(BF16)
-        copy = pltpu.make_async_copy(
-            out_s.at[pair_rows(p)], tgrad_hbm.at[pair_rows(p)], out_sem.at[1 + p]
-        )
-        copy.start()
-        return copy
+        tgrad_out[pair_rows(p), :] = (dz_s[pair_rows(p), :] + y_sum(DX_SUM, p)).astype(BF16)
 
     wq_load.wait()
     wk_load.wait()
@@ -627,88 +621,85 @@
     feed_forward_back(0)
     y_wait(F_SUM, 1)
     norm_two(1)
-    mixed_copy = pltpu.make_async_copy(out_s, mixed_hbm, out_sem.at[0])
-    mixed_copy.start()
+    outer_grad(2)
     outer_grad(1)
     outer_grad(0)
+    advance(2, 1)
+    advance(1, 1)
     feed_forward_back(1)
-    advance(1, 1)
     inner_grad(1)
     advance(0, 1)
-    outer_grad(2)
+    inner_grad(0)
+    advance(4, 1)
+    advance(3, 1)
+    advance(2, 2)
     inner_grad(2)
+    advance(1, 2)
+    y_wait(DH_SUM, 0)
+    norm_one_back(0)
+    attention_back(0)
+    inputs_back(0)
+    inputs_send(0)
+    advance(0, 2)
     ss0[...] = jnp.zeros(ss0.shape, F32)
     place_vector(ROW_G2, acc[A_G2])
     place_vector(ROW_S2, acc[A_S2])
     place_vector(ROW_BOUTER, acc[A_BOUTER])
     place_vector(ROW_BIN, accb[...])
-    inner_grad(0)
-    advance(2, 1)
-    advance(4, 1)
     advance(5, 1)
-    y_wait(DH_SUM, 0)
-    norm_one_back(0)
-    attention_back(0)
-    inputs_back(0)
-    inputs_send(0)
-    advance(1, 2)
-    advance(0, 2)
-    advance(3, 1)
-    advance(2, 2)
-    advance(5, 2)
+    advance(4, 2)
     advance(1, 3)
-    advance(4, 2)
+    advance(2, 3)
     y_wait(DH_SUM, 1)
     norm_one_back(1)
     weight_grad(OUT, df_s[...], att_all[:, att_mine])
+    advance(3, 2)
     attention_back(1)
-    advance(5, 3)
+    advance(4, 3)
+    advance(OUT, 1)
     qkv_grad(KEY)
+    advance(5, 2)
     qkv_grad(VALUE)
-    advance(OUT, 1)
-    complete(1)
-    advance(0, 3)
-    inputs_back(1)
-    send_document_sums()
-    inputs_send(1)
-    mixed_copy.wait()
+    qkv_grad(QUERY)
     advance(KEY, 1)
-    advance(4, 3)
-    advance(3, 2)
-    complete(5)
+    advance(3, 3)
+    complete(2)
     advance(VALUE, 1)
-    qkv_grad(QUERY)
-    advance(2, 3)
-    tgrad_copies = [input_grad(0)]
+    advance(QUERY, 1)
     place_vector(ROW_G1, acc[A_G1])
     place_vector(ROW_S1, acc[A_S1])
     place_vector(ROW_BOUT, acc[A_BOUT])
     place_vector(ROW_BQ, accq[0])
     place_vector(ROW_BV, accq[1])
     piece_copy(SMALL, 0).start()
-    complete(0)
+    advance(OUT, 2)
+    inputs_back(1)
+    send_document_sums()
+    inputs_send(1)
+    advance(5, 3)
+    advance(KEY, 2)
+    advance(VALUE, 2)
     send_document_parts()
-    advance(OUT, 2)
-    advance(QUERY, 1)
+    advance(OUT, 3)
     advance(SMALL, 1)
-    complete(4)
-    advance(3, 3)
-    advance(KEY, 2)
-    add_document_parts()
-    complete(2)
-    advance(OUT, 3)
-    advance(VALUE, 2)
+    advance(0, 3)
+    advance(QUERY, 2)
+    advance(VALUE, 3)
+    complete(1)
+    complete(5)
+    input_grad(0)
+    advance(SMALL, 2)
+    advance(KEY, 3)
     complete(3)
-    advance(KEY, 3)
-    tgrad_copies.append(input_grad(1))
-    advance(QUERY, 2)
-    complete(OUT)
-    advance(VALUE, 3)
-    advance(SMALL, 2)
-    complete(KEY)
     advance(QUERY, 3)
     advance(SMALL, 3)
+    input_grad(1)
+    complete(KEY)
+    add_document_parts()
+    complete(4)
+    complete(OUT)
     complete(VALUE)
+    complete(0)
     complete(QUERY)
     complete(SMALL)
     for copy in out_weight_copies:
@@ -725,33 +716,23 @@
             piece_copy(m, phase).wait_send()
     lax.fori_loop(1, n_batch, doc_sent, 0)
     lax.fori_loop(1, n_batch, part_sent, 0)
-    for copy in tgrad_copies:
-        copy.wait()
 
 
 def finish_kernel(
     local, mixed_ref, tgrad_ref, grads_ref, small_ref, docs_ref,
     mixed_out, tgrad_out, doc_out, wq_out, bq_out, wk_out, wv_out, bv_out, wo_out, bo_out,
     g1_out, s1_out, wi_out, bi_out, w2_out, b2_out, g2_out, s2_out,
-    rows_held, grads_held, in_sem, out_sem,
+    out_sem,
 ):
-    half = mixed_ref.shape[0] // 2
-    moves = []
-    for i, (source, target) in enumerate(((mixed_ref, mixed_out), (tgrad_ref, tgrad_out))):
-        for k in range(2):
-            part = pl.ds(k * half, half)
-            moves.append((source.at[part], rows_held.at[i, part], [(rows_held.at[i, part], target.at[part])]))
-    for m, targets in enumerate(((w2_out,), (wi_out,), (wo_out, wq_out, wk_out, wv_out))):
-        stores = [
-            (grads_held.at[m, :, pl.ds(n * local, local)] if m == 2 else grads_held.at[m], target)
-            for n, target in enumerate(targets)
-        ]
-        moves.append((grads_ref.at[m], grads_held.at[m], stores))
-    loads = [
-        pltpu.make_async_copy(source, held, in_sem.at[i])
-        for i, (source, held, _) in enumerate(moves)
+    moves = [(mixed_ref, mixed_out), (tgrad_ref, tgrad_out), (grads_ref.at[0], w2_out)]
+    moves.append((grads_ref.at[1], wi_out))
+    for n, target in enumerate((wo_out, wq_out, wk_out, wv_out)):
+        moves.append((grads_ref.at[2, :, pl.ds(n * local, local)], target))
+    copies = [
+        pltpu.make_async_copy(source, target, out_sem.at[i])
+        for i, (source, target) in enumerate(moves)
     ]
-    for copy in loads:
+    for copy in copies:
         copy.start()
     docs_dev, width = doc_out.shape
     for n in range(docs_dev):
@@ -763,13 +744,7 @@
         (ROW_S2, s2_out),
     ):
         out[...] = small_ref[row, 0 : out.shape[0]]
-    stored = []
-    for copy, (_, _, stores) in zip(loads, moves):
-        copy.wait()
-        for source, target in stores:
-            stored.append(pltpu.make_async_copy(source, target, out_sem.at[len(stored)]))
-            stored[-1].start()
-    for copy in stored:
+    for copy in copies:
         copy.wait()
 
 
@@ -803,7 +778,6 @@
         V((rows, hidden), BF16), V((rows, hidden), F32),
         V((rows, width), F32), V((rows, width), BF16), V((rows, hidden), BF16),
         V((rows, local), BF16), V((rows, 3 * local), BF16),
-        V((rows, width), BF16),
         V((6, 8, width), F32), V((8, hidden), F32), V((2, 8, local), F32),
         V((pairs, 8, width), F32),
         V((3, pairs, seq, width), BF16), V((3, pairs, seq, width), BF16),
@@ -815,20 +789,20 @@
         V((pairs, 8, LANES), F32), V((pairs, 8, LANES), F32),
         dma((3, pairs, 2)), dma((3, pairs, 2)), dma((pairs, local // LANES)),
         dma((pairs, local // LANES)), dma((3,)), dma((3,)), dma((11, 4)), dma((11, 4)),
-        dma((2, n_batch)), dma((2, n_batch)), dma((1,)), dma((1,)), dma((8,)), dma((1 + pairs,)),
+        dma((2, n_batch)), dma((2, n_batch)), dma((1,)), dma((1,)), dma((8,)),
     ]
     shape = jax.ShapeDtypeStruct
     mixed, tokens_grad, grads, small, docs = pl.pallas_call(
         functools.partial(layer_kernel, (n_batch, pairs, seq)),
         out_shape=(
-            shape((rows, width), BF16),
-            shape((rows, width), BF16),
-            shape((3, chunk, hidden), F32),
-            shape((SMALL_ROWS, LANES), F32),
-            shape((8 * docs_dev, LANES), F32),
+            V((rows, width), BF16),
+            V((rows, width), BF16),
+            V((3, chunk, hidden), F32),
+            V((SMALL_ROWS, LANES), F32),
+            V((8 * docs_dev, LANES), F32),
         ),
         in_specs=[hbm] * 8 + [vmem, smem] + [vmem] * 9,
-        out_specs=(hbm, hbm, vmem, vmem, vmem),
+        out_specs=(vmem,) * 5,
         scratch_shapes=scratch,
         compiler_params=pltpu.CompilerParams(
             collective_id=0, has_side_effects=True, vmem_limit_bytes=60 * 1024 * 1024
@@ -856,6 +830,11 @@
             pieces.append(jnp.pad(piece, (0, LANES - size)))
         small = jnp.stack(pieces)
 
+    if inner == 1:
+        mixed, tokens_grad, grads, small, docs = (
+            pltpu.with_memory_space_constraint(item, pltpu.VMEM)
+            for item in (mixed, tokens_grad, grads, small, docs)
+        )
     out_rows = width // n_batch
     vector = shape((out_rows,), F32)
     vector_local = shape((local // n_batch,), F32)
@@ -872,14 +851,12 @@
             shape((out_rows, hidden), F32), shape((hidden // n_batch,), F32),
             shape((out_rows, hidden), F32), vector, vector, vector,
         ),
-        in_specs=[hbm, hbm, hbm, vmem, vmem],
+        in_specs=[vmem] * 5,
         out_specs=(
             hbm, hbm, vmem, hbm, vmem, hbm, hbm, vmem, hbm, vmem, vmem, vmem, hbm, vmem, hbm,
             vmem, vmem, vmem,
         ),
-        scratch_shapes=[
-            V((2, rows, width), BF16), V((3, out_rows, hidden), F32), dma((7,)), dma((10,)),
-        ],
+        scratch_shapes=[dma((8,))],
         name="gradient_outputs",
     )(mixed, tokens_grad, grads, small, docs)
     return (

time: 103 us -> 96.3 us (0.935)
  Pallas kernels: 102 us -> 95.2 us
    pallas_call x1, Pallas kernels: 98.2 us -> 93.1 us  [body(): pl.pallas_call(functools.partial(layer_kernel, (n_batch, pairs, seq)), ou...]
    pallas_call x1, Pallas kernels: 3.99 us -> 2.19 us  [body(): pl.pallas_call(functools.partial(finish_kernel, local), out_shape=(shape(...]
where the time goes in v3:
time: 96.3 us; the launch traced here: 96.1 us
  Pallas kernels  95.2 us (99%)
    pallas_call x1, Pallas kernels, body(): pl.pallas_call(functools.partial(layer_kernel, (n_batch, pairs, seq)), ou...  93.1 us
    pallas_call x1, Pallas kernels, body(): pl.pallas_call(functools.partial(finish_kernel, local), out_shape=(shape(...  2.19 us

profile of v3, /device:TPU:0, one launch (start us, length us, event | category | flops | bytes accessed | tf_op | source)
XLA Modules:
  0.0 96.1 jit_solution(3032245108556257737)
XLA Ops:
  0.7 93.1 %encoder_layer.1 = (bf16[576,768]{1,0:T(8,128)(2,1)S(1)}, bf16[576,768]{1,0:T(8,128)(2,1)S(1)}, f32[3,48,1536]{2,1,0:T(8,128)S(1)}, f32[16,128]{1,0:T(8,128)S(1)}, f32[16,128]{1,0:T(8,128)S(1)}) custom-call(bf16[576,768]{1,0:T(8,128)(2,1)} %tokens_hbm.1, bf16[576,768]{1,0:T(8,128)(2,1)} %cot_hbm.1, bf16[768,384]{1,0:T(8,128)(2,1)} %wq_hbm.1, ...), custom_call_target="tpu_custom_call" | custom-call | tf_op jit(solution)/shard_map/encoder_layer/pallas_call | solution.py:795
  93.7 2.2 %gradient_outputs.1 = (bf16[576,768]{1,0:T(8,128)(2,1)}, bf16[576,768]{1,0:T(8,128)(2,1)}, f32[2,768]{1,0:T(2,128)}, f32[48,384]{1,0:T(8,128)}, f32[24]{0:T(128)...) custom-call(bf16[576,768]{1,0:T(8,128)(2,1)S(1)} %get-tuple-element., ...), custom_call_target="tpu_custom_call" | custom-call | tf_op jit(solution)/shard_map/gradient_outputs/pallas_call | solution.py:845

commit v4 on v3

--- a/solution.py
+++ b/solution.py
@@ -38,12 +38,14 @@
 def layer_kernel(
     sizes,
     tokens_hbm, cot_hbm, wq_hbm, wk_hbm, wv_hbm, wo_hbm, wi_hbm, w2_hbm,
+    docs_hbm, ids_hbm, bq_hbm, bv_hbm, bo_hbm, g1_hbm, s1_hbm, bi_hbm, b2_hbm, g2_hbm, s2_hbm,
+    mixed_out, tgrad_out, grads_out, small_out, docs_out,
     docs_ref, ids_ref, bq_ref, bv_ref, bo_ref, g1_ref, s1_ref, bi_ref, b2_ref, g2_ref, s2_ref,
-    mixed_out, tgrad_out, grads_out, small_out, docs_out,
     tok, cot, w_qkv, wo_all, wi, w2,
     x_low, qkv_s, p_s, att_all, n1_s, r1_s, h1_low, g_s, sl_s, dz_s, df_s, du_s,
     da_s, dqkv_s, acc, accb, accq, accx,
-    y_send, y_recv, ff0, ff1, ff2, ff3, ff4, at0, at1, at2, at3, at4, ss0, ss1, ss2, ss3, ss4,
+    y_send, y_recv, ff0, ff1, ff2, ff3, ff4, at0, at1, at2, at3, at4,
+    va0, va1, va2, va3, va4, vb0, vb1, vb2, vb3, vb4, ss0, ss1, ss2, ss3, ss4,
     doc_stage, doc_table, doc_part, doc_in, sum_send, sum_recv,
     y_ssem, y_rsem, a_ssem, a_rsem, w_ssem, w_rsem, r_ssem, r_rsem, d_ssem, d_rsem,
     s_ssem, s_rsem, load_sem,
@@ -78,29 +80,53 @@
     def batch_peer(step):
         return ((b + step) % n_batch, t)
 
+    def doc_steps(step):
+        if n_batch <= GROUP:
+            for i in range(1, n_batch):
+                step(i, 0)
+        else:
+            lax.fori_loop(1, n_batch, step, 0)
+
     barrier = pltpu.get_barrier_semaphore()
 
     def greet(step, carry):
         pl.semaphore_signal(barrier, inc=1, device_id=batch_peer(step), device_id_type=MESH)
         return carry
 
-    lax.fori_loop(1, n_batch, greet, 0)
+    doc_steps(greet)
     pl.semaphore_signal(barrier, inc=1, device_id=y_peer, device_id_type=MESH)
 
     wo_mine = pl.ds(pl.multiple_of(t * local, LANES), local)
     att_mine = wo_mine
     loads = []
+    vectors = (
+        (bq_hbm, bq_ref), (bv_hbm, bv_ref), (bo_hbm, bo_ref), (g1_hbm, g1_ref), (s1_hbm, s1_ref),
+        (bi_hbm, bi_ref), (b2_hbm, b2_ref), (g2_hbm, g2_ref), (s2_hbm, s2_ref),
+    )
+    head_pairs = local // LANES
+    group = 3 * LANES
+    qkv_weights = [
+        (
+            source.at[:, pl.ds(j * LANES, LANES)],
+            w_qkv.at[:, pl.ds(j * group + kind * LANES, LANES)],
+        )
+        for j in range(head_pairs)
+        for kind, source in enumerate((wq_hbm, wk_hbm, wv_hbm))
+    ]
     for i, (src, dst) in enumerate(
         (
-            (tokens_hbm, tok), (wq_hbm, w_qkv.at[:, 0:local]),
-            (wk_hbm, w_qkv.at[:, local : 2 * local]), (wv_hbm, w_qkv.at[:, 2 * local :]),
+            (docs_hbm, docs_ref), (ids_hbm, ids_ref), *vectors,
+            (tokens_hbm, tok), *qkv_weights,
             (wo_hbm, wo_all.at[wo_mine]), (wi_hbm, wi), (w2_hbm, w2), (cot_hbm, cot),
         )
     ):
         copy = pltpu.make_async_copy(src, dst, load_sem.at[i])
         copy.start()
         loads.append(copy)
-    (tok_load, wq_load, wk_load, wv_load, wo_load, wi_load, w2_load, cot_load) = loads
+    docs_load, ids_load = loads[:2]
+    tok_load, *qkv_loads = loads[2 + len(vectors) : -4]
+    wo_load, wi_load, w2_load, cot_load = loads[-4:]
+    docs_load.wait()
 
     doc_rows = docs_ref[...].astype(F32)
     pieces = []
@@ -113,22 +139,6 @@
     stage = jnp.concatenate(pieces, axis=0).astype(BF16)
     doc_stage[...] = stage
     doc_table[b] = stage
-
-    b_qkv = jnp.concatenate(
-        [
-            bq_ref[...].astype(F32).reshape(1, local),
-            jnp.zeros((1, local), F32),
-            bv_ref[...].astype(F32).reshape(1, local),
-        ],
-        axis=1,
-    )
-    b_out = bo_ref[...].astype(F32).reshape(1, width)
-    gain1 = g1_ref[...].astype(F32).reshape(1, width)
-    shift1 = s1_ref[...].astype(F32).reshape(1, width)
-    b_inner = bi_ref[...].astype(F32).reshape(1, hidden)
-    b_outer = b2_ref[...].astype(F32).reshape(1, width)
-    gain2 = g2_ref[...].astype(F32).reshape(1, width)
-    shift2 = s2_ref[...].astype(F32).reshape(1, width)
 
     pl.semaphore_wait(barrier, n_batch)
 
@@ -203,11 +213,24 @@
         doc_copy(step).wait_send()
         return carry
 
-    lax.fori_loop(1, n_batch, doc_start, 0)
+    doc_steps(doc_start)
+
+    for copy in loads[2 : 2 + len(vectors)]:
+        copy.wait()
+    b_query = bq_ref[...].astype(F32).reshape(1, local)
+    b_value = bv_ref[...].astype(F32).reshape(1, local)
+    b_out = bo_ref[...].astype(F32).reshape(1, width)
+    gain1 = g1_ref[...].astype(F32).reshape(1, width)
+    shift1 = s1_ref[...].astype(F32).reshape(1, width)
+    b_inner = bi_ref[...].astype(F32).reshape(1, hidden)
+    b_outer = b2_ref[...].astype(F32).reshape(1, width)
+    gain2 = g2_ref[...].astype(F32).reshape(1, width)
+    shift2 = s2_ref[...].astype(F32).reshape(1, width)
 
     tok_load.wait()
-    lax.fori_loop(1, n_batch, doc_wait, 0)
-
+    doc_steps(doc_wait)
+
+    ids_load.wait()
     ids = [jnp.full((8, LANES), ids_ref[p], jnp.int32) for p in range(pairs)]
 
     def pick(d, found):
@@ -298,24 +321,35 @@
         qkv_s[mine, :] = (product(x_low[mine, :], w_qkv[...]) + b_qkv).astype(BF16)
 
     def qkv(kind, j):
-        return pl.ds(kind * local + j * LANES, LANES)
-
-    def attention(p):
+        return pl.ds(j * group + kind * LANES, LANES)
+
+    def make_inputs(p):
+        x_low[pair_rows(p), :] = inputs_of(p).astype(BF16)
+
+    def attention(p, j):
         mine = pair_rows(p)
-        for j in range(local // LANES):
-            kk, vv = qkv_s[mine, qkv(1, j)], qkv_s[mine, qkv(2, j)]
-            qq = (qkv_s[mine, qkv(0, j)].astype(F32) * 0.125).astype(BF16)
-            qkv_s[mine, qkv(0, j)] = qq
-            low = []
-            for h in range(2):
-                scores = product(head_lanes(qq, h), kk, 1, 1)
-                expo = jnp.exp(scores - jnp.max(scores, axis=1, keepdims=True))
-                probs = expo * (1.0 / jnp.sum(expo, axis=1, keepdims=True))
-                p_s[p * (local // HEAD_DIM) + 2 * j + h] = probs
-                low.append(probs.astype(BF16))
-            both = product(low[0], head_lanes(vv, 0)) + product(low[1], head_lanes(vv, 1))
-            att_all[mine, att_cols(t, j)] = both.astype(BF16)
-            att_copy(p, j).start()
+        here = pl.ds(j * LANES, LANES)
+        if p == 0:
+            for copy in qkv_loads[3 * j : 3 * j + 3]:
+                copy.wait()
+        both = product(x_low[mine, :], w_qkv[:, pl.ds(j * group, group)])
+        qq = (both[:, 0:LANES] + b_query[:, j * LANES : (j + 1) * LANES]).astype(BF16)
+        qq = (qq.astype(F32) * 0.125).astype(BF16)
+        kk = both[:, LANES : 2 * LANES].astype(BF16)
+        vv = (both[:, 2 * LANES :] + b_value[:, j * LANES : (j + 1) * LANES]).astype(BF16)
+        qkv_s[mine, qkv(0, j)] = qq
+        qkv_s[mine, qkv(1, j)] = kk
+        qkv_s[mine, qkv(2, j)] = vv
+        low = []
+        for h in range(2):
+            scores = product(head_lanes(qq, h), kk, 1, 1)
+            expo = jnp.exp(scores - jnp.max(scores, axis=1, keepdims=True))
+            probs = expo * (1.0 / jnp.sum(expo, axis=1, keepdims=True))
+            p_s[p * (local // HEAD_DIM) + 2 * j + h] = probs
+            low.append(probs.astype(BF16))
+        out = product(low[0], head_lanes(vv, 0)) + product(low[1], head_lanes(vv, 1))
+        att_all[mine, att_cols(t, j)] = out.astype(BF16)
+        att_copy(p, j).start()
 
     def attention_out(p):
         for j in range(local // LANES):
@@ -388,31 +422,37 @@
         add_acc(A_S1, p, fold_rows(dh))
         add_acc(A_BOUT, p, doc_part_rows + fold_rows(dz[:QLEN, :]))
 
-    def attention_back(p):
+    def attended_back(p):
         mine = pair_rows(p)
         da_s[mine, :] = product(df_s[mine, :], wo_all[wo_mine, :], 1, 1).astype(BF16)
-        for j in range(local // LANES):
-            qq, kk, vv = (qkv_s[mine, qkv(kind, j)] for kind in range(3))
-            dd = da_s[mine, pl.ds(j * LANES, LANES)]
-            low, ds = [], []
-            for h in range(2):
-                probs = p_s[p * (local // HEAD_DIM) + 2 * j + h]
-                low.append(probs.astype(BF16))
-                dp = product(head_lanes(dd, h), vv, 1, 1)
-                slope = probs * (dp - jnp.sum(probs * dp, axis=1, keepdims=True))
-                ds.append(slope.astype(BF16))
-            dv = product(jnp.concatenate(low, axis=0), both_heads(dd), 0, 0)
-            dk = product(jnp.concatenate(ds, axis=0), both_heads(qq), 0, 0)
-            dq = product(ds[0], head_lanes(kk, 0)) + product(ds[1], head_lanes(kk, 1))
-            dqkv_s[mine, qkv(0, j)] = (dq * 0.125).astype(BF16)
-            dqkv_s[mine, qkv(1, j)] = dk.astype(BF16)
-            dqkv_s[mine, qkv(2, j)] = dv.astype(BF16)
-        for i, kind in enumerate((0, 2)):
-            total = fold_rows(dqkv_s[mine, pl.ds(kind * local, local)].astype(F32))
-            if p == 0:
-                accq[i] = total
-            else:
-                accq[i] = accq[i] + total
+
+    def heads_back(p, j):
+        mine = pair_rows(p)
+        qq, kk, vv = (qkv_s[mine, qkv(kind, j)] for kind in range(3))
+        dd = da_s[mine, pl.ds(j * LANES, LANES)]
+        low, ds = [], []
+        for h in range(2):
+            probs = p_s[p * (local // HEAD_DIM) + 2 * j + h]
+            low.append(probs.astype(BF16))
+            dp = product(head_lanes(dd, h), vv, 1, 1)
+            slope = probs * (dp - jnp.sum(probs * dp, axis=1, keepdims=True))
+            ds.append(slope.astype(BF16))
+        dv = product(jnp.concatenate(low, axis=0), both_heads(dd), 0, 0).astype(BF16)
+        dk = product(jnp.concatenate(ds, axis=0), both_heads(qq), 0, 0)
+        dq = product(ds[0], head_lanes(kk, 0)) + product(ds[1], head_lanes(kk, 1))
+        dq = (dq * 0.125).astype(BF16)
+        dqkv_s[mine, qkv(0, j)] = dq
+        dqkv_s[mine, qkv(1, j)] = dk.astype(BF16)
+        dqkv_s[mine, qkv(2, j)] = dv
+        cols = pl.ds(j * LANES, LANES)
+        for i, value in enumerate((dq, dv)):
+            total = fold_rows(value.astype(F32))
+            accq[i, :, cols] = total if p == 0 else accq[i, :, cols] + total
+
+    def attention_back(p):
+        attended_back(p)
+        for j in range(head_pairs):
+            heads_back(p, j)
 
     def inputs_back(p):
         mine = pair_rows(p)
@@ -425,15 +465,21 @@
             y_copy(DX_SUM, p, part).start()
 
     N_FF = 6
-    N_PIECES = 11
+    N_PIECES = 12
+    OUT, HEADS, HEADS_MID, HEADS_END, HEADS_LAST, SMALL = range(N_FF, N_PIECES)
+    value_split = va0.shape[-1]
     X_Z, Z_X_Z, Z_Z_X = (0, 1, 2, 3), (0, 2, 1, 3), (0, 2, 3, 1)
-    HALVING = (Z_Z_X, X_Z, Z_Z_X, X_Z, X_Z, X_Z, X_Z, X_Z, X_Z, Z_X_Z, X_Z)
+    HALVING = (X_Z, X_Z, Z_Z_X, X_Z, X_Z, Z_Z_X, X_Z, X_Z, X_Z, X_Z, Z_X_Z, X_Z)
 
     def piece_refs(m):
         if m < N_FF:
             return [ref.at[m] for ref in (ff0, ff1, ff2, ff3, ff4)]
-        if m < N_PIECES - 1:
+        if m < HEADS_END:
             return [ref.at[m - N_FF] for ref in (at0, at1, at2, at3, at4)]
+        if m == HEADS_END:
+            return [va0, va1, va2, va3, va4]
+        if m == HEADS_LAST:
+            return [vb0, vb1, vb2, vb3, vb4]
         return [ss0, ss1, ss2, ss3, ss4]
 
     def chunk_index(m, r):
@@ -481,9 +527,14 @@
         total = refs[0][index].astype(F32) + refs[4][...].astype(F32)
         if m < N_FF:
             grads_out[m // 3, :, (m % 3) * FF_TILE : (m % 3 + 1) * FF_TILE] = total
-        elif m < N_PIECES - 1:
-            n = m - N_FF
-            grads_out[2, :, n * local : (n + 1) * local] = total
+        elif m == OUT:
+            grads_out[2, :, 0:local] = total
+        elif m < SMALL:
+            j = min(m - HEADS, 2)
+            for k in range(total.shape[1] // LANES):
+                kind = k if m < HEADS_LAST else k + value_split // LANES
+                first = (1 + kind) * local + j * LANES
+                grads_out[2, :, first : first + LANES] = total[:, k * LANES : (k + 1) * LANES]
         else:
             small_out[...] = total
 
@@ -508,11 +559,25 @@
                 :, r * piece : (r + 1) * piece
             ]
 
-    OUT, QUERY, KEY, VALUE, SMALL = range(N_FF, N_PIECES)
-
-    def qkv_grad(m):
-        kind = m - QUERY
-        weight_grad(m, x_low[...], dqkv_s[:, kind * local : (kind + 1) * local])
+    def heads_grad(m):
+        first = (m - HEADS) * group if m < HEADS_LAST else 2 * group + value_split
+        last = {HEADS_END: 2 * group + value_split, HEADS_LAST: 3 * group}.get(m, first + group)
+        weight_grad(m, x_low[...], dqkv_s[:, first:last])
+
+    def sent_early():
+        for copy in out_weight_copies:
+            copy.wait_send()
+        for p in range(pairs):
+            for j in range(local // LANES):
+                att_copy(p, j).wait_send()
+        doc_steps(doc_sent)
+
+    def sent_late():
+        sum_copy.wait_send()
+        doc_steps(part_sent)
+        for m in range(N_PIECES - 1):
+            for phase in range(3 if m < N_FF else 2):
+                piece_copy(m, phase).wait_send()
 
     zero_row = jnp.zeros((1, LANES), F32)
     sum_copy = pltpu.make_async_remote_copy(
@@ -581,11 +646,11 @@
             return carry
 
         lax.fori_loop(0, n_batch, fill, 0)
-        lax.fori_loop(1, n_batch, part_start, 0)
+        doc_steps(part_start)
         doc_in[b] = doc_part[b]
 
     def add_document_parts():
-        lax.fori_loop(1, n_batch, part_wait, 0)
+        doc_steps(part_wait)
 
         def add_part(d, total):
             return total + doc_in[d]
@@ -596,17 +661,18 @@
         y_wait(DX_SUM, p)
         tgrad_out[pair_rows(p), :] = (dz_s[pair_rows(p), :] + y_sum(DX_SUM, p)).astype(BF16)
 
-    wq_load.wait()
-    wk_load.wait()
-    wv_load.wait()
-    project(0)
+    make_inputs(0)
+    attention(0, 0)
     out_weight_copies[0].wait_recv()
     out_weight_copies[1].start()
-    attention(0)
-    project(1)
-    attention(1)
+    attention(0, 1)
+    attention(0, 2)
+    make_inputs(1)
+    attention(1, 0)
+    attention(1, 1)
     out_weight_copies[1].wait_recv()
     out_weight_copies[2].start()
+    attention(1, 2)
     wo_load.wait()
     out_weight_copies[2].wait_recv()
     wi_load.wait()
@@ -615,107 +681,111 @@
     feed_forward(0)
     attention_out(1)
     feed_forward(1)
+    sent_early()
     cot_load.wait()
     y_wait(F_SUM, 0)
     norm_two(0)
     feed_forward_back(0)
     y_wait(F_SUM, 1)
     norm_two(1)
+    outer_grad(1)
     outer_grad(2)
-    outer_grad(1)
+    feed_forward_back(1)
+    advance(2, 1)
+    inner_grad(1)
+    advance(1, 1)
+    inner_grad(2)
+    advance(5, 1)
     outer_grad(0)
-    advance(2, 1)
-    advance(1, 1)
-    feed_forward_back(1)
-    inner_grad(1)
-    advance(0, 1)
+    advance(4, 1)
     inner_grad(0)
-    advance(4, 1)
+    advance(2, 2)
+    ss0[...] = jnp.zeros(ss0.shape, F32)
+    place_vector(ROW_G2, acc[A_G2])
+    place_vector(ROW_S2, acc[A_S2])
+    place_vector(ROW_BOUTER, acc[A_BOUTER])
+    place_vector(ROW_BIN, accb[...])
     advance(3, 1)
-    advance(2, 2)
-    inner_grad(2)
     advance(1, 2)
     y_wait(DH_SUM, 0)
     norm_one_back(0)
     attention_back(0)
     inputs_back(0)
     inputs_send(0)
-    advance(0, 2)
-    ss0[...] = jnp.zeros(ss0.shape, F32)
-    place_vector(ROW_G2, acc[A_G2])
-    place_vector(ROW_S2, acc[A_S2])
-    place_vector(ROW_BOUTER, acc[A_BOUTER])
-    place_vector(ROW_BIN, accb[...])
-    advance(5, 1)
+    advance(5, 2)
     advance(4, 2)
-    advance(1, 3)
-    advance(2, 3)
+    advance(0, 1)
     y_wait(DH_SUM, 1)
     norm_one_back(1)
     weight_grad(OUT, df_s[...], att_all[:, att_mine])
+    advance(1, 3)
     advance(3, 2)
-    attention_back(1)
+    attended_back(1)
+    heads_back(1, 0)
+    advance(OUT, 1)
+    heads_grad(HEADS)
     advance(4, 3)
-    advance(OUT, 1)
-    qkv_grad(KEY)
-    advance(5, 2)
-    qkv_grad(VALUE)
-    qkv_grad(QUERY)
-    advance(KEY, 1)
+    heads_back(1, 1)
+    heads_grad(HEADS_MID)
+    advance(0, 2)
+    advance(HEADS, 1)
+    heads_back(1, 2)
+    complete(1)
+    heads_grad(HEADS_LAST)
+    advance(HEADS_MID, 1)
     advance(3, 3)
-    complete(2)
-    advance(VALUE, 1)
-    advance(QUERY, 1)
+    advance(HEADS_LAST, 1)
+    heads_grad(HEADS_END)
+    advance(OUT, 2)
+    inputs_back(1)
+    send_document_sums()
+    inputs_send(1)
     place_vector(ROW_G1, acc[A_G1])
     place_vector(ROW_S1, acc[A_S1])
     place_vector(ROW_BOUT, acc[A_BOUT])
     place_vector(ROW_BQ, accq[0])
     place_vector(ROW_BV, accq[1])
     piece_copy(SMALL, 0).start()
-    advance(OUT, 2)
-    inputs_back(1)
-    send_document_sums()
-    inputs_send(1)
-    advance(5, 3)
-    advance(KEY, 2)
-    advance(VALUE, 2)
+    advance(0, 3)
+    advance(SMALL, 1)
+    advance(HEADS, 2)
+    advance(HEADS_END, 1)
+    advance(HEADS_LAST, 2)
+    advance(2, 3)
     send_document_parts()
     advance(OUT, 3)
-    advance(SMALL, 1)
-    advance(0, 3)
-    advance(QUERY, 2)
-    advance(VALUE, 3)
-    complete(1)
+    advance(HEADS_MID, 2)
+    advance(SMALL, 2)
+    complete(4)
+    advance(HEADS, 3)
+    complete(3)
+    advance(5, 3)
+    advance(HEADS_END, 2)
+    advance(HEADS_LAST, 3)
+    advance(HEADS_MID, 3)
+    input_grad(0)
+    advance(SMALL, 3)
     complete(5)
-    input_grad(0)
-    advance(SMALL, 2)
-    advance(KEY, 3)
-    complete(3)
-    advance(QUERY, 3)
-    advance(SMALL, 3)
+    complete(0)
+    advance(HEADS_END, 3)
+    add_document_parts()
+    complete(HEADS_LAST)
+    sent_late()
     input_grad(1)
-    complete(KEY)
-    add_document_parts()
-    complete(4)
+    complete(HEADS_MID)
+    complete(2)
+    complete(SMALL)
     complete(OUT)
-    complete(VALUE)
-    complete(0)
-    complete(QUERY)
-    complete(SMALL)
-    for copy in out_weight_copies:
-        copy.wait_send()
-    sum_copy.wait_send()
+    complete(HEADS)
+    complete(HEADS_END)
     for p in range(pairs):
-        for j in range(local // LANES):
-            att_copy(p, j).wait_send()
-        for kind in range(3):
-            for part in range(2):
-                y_copy(kind, p, part).wait_send()
+        for part in range(2):
+            y_copy(DX_SUM, p, part).wait_send()
+            y_copy(F_SUM, p, part).wait_send()
+            y_copy(DH_SUM, p, part).wait_send()
     for m in range(N_PIECES):
-        for phase in range(4):
+        for phase in range(3 if m < N_FF else 2 if m < SMALL else 0, 4):
             piece_copy(m, phase).wait_send()
-    lax.fori_loop(1, n_batch, doc_sent, 0)
-    lax.fori_loop(1, n_batch, part_sent, 0)
 
 
 def finish_kernel(
@@ -762,12 +832,17 @@
     docs_dev = doc_vectors.shape[0]
     chunk = width // GROUP
     part = hidden // 3
+    split = local * 2 // 3 // LANES * LANES
     hbm = pl.BlockSpec(memory_space=pl.ANY)
     vmem = pl.BlockSpec(memory_space=pltpu.VMEM)
-    smem = pl.BlockSpec(memory_space=pltpu.SMEM)
     V = pltpu.VMEM
     dma = pltpu.SemaphoreType.DMA
+    smalls = (
+        b_query, b_value, b_out, gain_one, shift_one, b_inner, b_outer, gain_two, shift_two,
+    )
     scratch = [
+        V(doc_vectors.shape, BF16), pltpu.SMEM(doc_ids.shape, jnp.int32),
+        *[V(item.shape, BF16) for item in smalls],
         V((rows, width), BF16), V((rows, width), BF16),
         V((width, 3 * local), BF16), V((width, width), BF16), V((width, hidden), BF16), V((hidden, width), BF16),
         V((rows, width), BF16),
@@ -782,14 +857,16 @@
         V((pairs, 8, width), F32),
         V((3, pairs, seq, width), BF16), V((3, pairs, seq, width), BF16),
         *[V((6, *(2,) * n, chunk, part), BF16) for n in (4, 3, 2, 1, 0)],
-        *[V((4, *(2,) * n, chunk, local), BF16) for n in (4, 3, 2, 1, 0)],
+        *[V((3, *(2,) * n, chunk, local), BF16) for n in (4, 3, 2, 1, 0)],
+        *[V((*(2,) * n, chunk, split), BF16) for n in (4, 3, 2, 1, 0)],
+        *[V((*(2,) * n, chunk, local - split), BF16) for n in (4, 3, 2, 1, 0)],
         *[V((*(2,) * n, SMALL_ROWS, LANES), F32) for n in (4, 3, 2, 1, 0)],
         V((8 * docs_dev, LANES), BF16), V((n_batch, 8 * docs_dev, LANES), BF16),
         V((n_batch, 8 * docs_dev, LANES), F32), V((n_batch, 8 * docs_dev, LANES), F32),
         V((pairs, 8, LANES), F32), V((pairs, 8, LANES), F32),
         dma((3, pairs, 2)), dma((3, pairs, 2)), dma((pairs, local // LANES)),
-        dma((pairs, local // LANES)), dma((3,)), dma((3,)), dma((11, 4)), dma((11, 4)),
-        dma((2, n_batch)), dma((2, n_batch)), dma((1,)), dma((1,)), dma((8,)),
+        dma((pairs, local // LANES)), dma((3,)), dma((3,)), dma((12, 4)), dma((12, 4)),
+        dma((2, n_batch)), dma((2, n_batch)), dma((1,)), dma((1,)), dma((25,)),
     ]
     shape = jax.ShapeDtypeStruct
     mixed, tokens_grad, grads, small, docs = pl.pallas_call(
@@ -801,7 +878,7 @@
             V((SMALL_ROWS, LANES), F32),
             V((8 * docs_dev, LANES), F32),
         ),
-        in_specs=[hbm] * 8 + [vmem, smem] + [vmem] * 9,
+        in_specs=[hbm] * 19,
         out_specs=(vmem,) * 5,
         scratch_shapes=scratch,
         compiler_params=pltpu.CompilerParams(
@@ -810,8 +887,7 @@
         name="encoder_layer",
     )(
         tokens, cotangent, w_query, w_key, w_value, w_out, w_inner, w_outer,
-        doc_vectors, doc_ids, b_query, b_value, b_out, gain_one, shift_one, b_inner, b_outer,
-        gain_two, shift_two,
+        doc_vectors, doc_ids, *smalls,
     )
 
     inner = n_batch // GROUP

time: 96.3 us -> 94.3 us (0.979)
  Pallas kernels: 95.2 us -> 93.2 us
    pallas_call x1, Pallas kernels: 93.1 us -> 91 us  [body(): pl.pallas_call(functools.partial(layer_kernel, (n_batch, pairs, seq)), ou...]
where the time goes in v4:
time: 94.3 us; the launch traced here: 94.1 us
  Pallas kernels  93.2 us (99%)
    pallas_call x1, Pallas kernels, body(): pl.pallas_call(functools.partial(layer_kernel, (n_batch, pairs, seq)), ou...  91 us
    pallas_call x1, Pallas kernels, body(): pl.pallas_call(functools.partial(finish_kernel, local), out_shape=(shape(...  2.19 us

profile of v4, /device:TPU:0, one launch (start us, length us, event | category | flops | bytes accessed | tf_op | source)
XLA Modules:
  0.0 94.1 jit_solution(14552246750344917202)
XLA Ops:
  0.7 91.0 %encoder_layer.1 = (bf16[576,768]{1,0:T(8,128)(2,1)S(1)}, bf16[576,768]{1,0:T(8,128)(2,1)S(1)}, f32[3,48,1536]{2,1,0:T(8,128)S(1)}, f32[16,128]{1,0:T(8,128)S(1)}, f32[16,128]{1,0:T(8,128)S(1)}) custom-call(bf16[576,768]{1,0:T(8,128)(2,1)} %tokens_hbm.1, bf16[576,768]{1,0:T(8,128)(2,1)} %cot_hbm.1, bf16[768,384]{1,0:T(8,128)(2,1)} %wq_hbm.1, ...), custom_call_target="tpu_custom_call" | custom-call | tf_op jit(solution)/shard_map/encoder_layer/pallas_call | solution.py:872
  91.7 2.2 %gradient_outputs.1 = (bf16[576,768]{1,0:T(8,128)(2,1)}, bf16[576,768]{1,0:T(8,128)(2,1)}, f32[2,768]{1,0:T(2,128)}, f32[48,384]{1,0:T(8,128)}, f32[24]{0:T(128)...) custom-call(bf16[576,768]{1,0:T(8,128)(2,1)S(1)} %get-tuple-element., ...), custom_call_target="tpu_custom_call" | custom-call | tf_op jit(solution)/shard_map/gradient_outputs/pallas_call | solution.py:921

commit v5 on v4

--- a/solution.py
+++ b/solution.py
@@ -469,7 +469,7 @@
     OUT, HEADS, HEADS_MID, HEADS_END, HEADS_LAST, SMALL = range(N_FF, N_PIECES)
     value_split = va0.shape[-1]
     X_Z, Z_X_Z, Z_Z_X = (0, 1, 2, 3), (0, 2, 1, 3), (0, 2, 3, 1)
-    HALVING = (X_Z, X_Z, Z_Z_X, X_Z, X_Z, Z_Z_X, X_Z, X_Z, X_Z, X_Z, Z_X_Z, X_Z)
+    HALVING = (X_Z, X_Z, Z_Z_X, X_Z, Z_Z_X, X_Z, X_Z, X_Z, X_Z, X_Z, Z_X_Z, X_Z)
 
     def piece_refs(m):
         if m < N_FF:
@@ -670,9 +670,9 @@
     make_inputs(1)
     attention(1, 0)
     attention(1, 1)
+    attention(1, 2)
     out_weight_copies[1].wait_recv()
     out_weight_copies[2].start()
-    attention(1, 2)
     wo_load.wait()
     out_weight_copies[2].wait_recv()
     wi_load.wait()
@@ -688,95 +688,95 @@
     feed_forward_back(0)
     y_wait(F_SUM, 1)
     norm_two(1)
+    outer_grad(2)
     outer_grad(1)
-    outer_grad(2)
+    advance(2, 1)
     feed_forward_back(1)
-    advance(2, 1)
+    advance(1, 1)
     inner_grad(1)
-    advance(1, 1)
     inner_grad(2)
-    advance(5, 1)
     outer_grad(0)
     advance(4, 1)
-    inner_grad(0)
-    advance(2, 2)
     ss0[...] = jnp.zeros(ss0.shape, F32)
     place_vector(ROW_G2, acc[A_G2])
     place_vector(ROW_S2, acc[A_S2])
     place_vector(ROW_BOUTER, acc[A_BOUTER])
     place_vector(ROW_BIN, accb[...])
-    advance(3, 1)
-    advance(1, 2)
+    advance(5, 1)
+    inner_grad(0)
+    advance(0, 1)
+    advance(2, 2)
     y_wait(DH_SUM, 0)
     norm_one_back(0)
     attention_back(0)
     inputs_back(0)
     inputs_send(0)
+    advance(1, 2)
+    advance(3, 1)
+    advance(4, 2)
     advance(5, 2)
-    advance(4, 2)
-    advance(0, 1)
     y_wait(DH_SUM, 1)
     norm_one_back(1)
     weight_grad(OUT, df_s[...], att_all[:, att_mine])
     advance(1, 3)
-    advance(3, 2)
+    advance(0, 2)
     attended_back(1)
     heads_back(1, 0)
     advance(OUT, 1)
     heads_grad(HEADS)
-    advance(4, 3)
     heads_back(1, 1)
+    advance(5, 3)
+    heads_back(1, 2)
+    advance(3, 2)
+    advance(HEADS, 1)
+    heads_grad(HEADS_LAST)
     heads_grad(HEADS_MID)
-    advance(0, 2)
-    advance(HEADS, 1)
-    heads_back(1, 2)
-    complete(1)
-    heads_grad(HEADS_LAST)
-    advance(HEADS_MID, 1)
-    advance(3, 3)
-    advance(HEADS_LAST, 1)
-    heads_grad(HEADS_END)
-    advance(OUT, 2)
-    inputs_back(1)
-    send_document_sums()
-    inputs_send(1)
     place_vector(ROW_G1, acc[A_G1])
     place_vector(ROW_S1, acc[A_S1])
     place_vector(ROW_BOUT, acc[A_BOUT])
     place_vector(ROW_BQ, accq[0])
     place_vector(ROW_BV, accq[1])
     piece_copy(SMALL, 0).start()
+    complete(1)
+    advance(HEADS_LAST, 1)
     advance(0, 3)
+    advance(HEADS_MID, 1)
+    advance(OUT, 2)
     advance(SMALL, 1)
+    heads_grad(HEADS_END)
+    complete(5)
+    inputs_back(1)
+    send_document_sums()
+    inputs_send(1)
+    advance(HEADS_END, 1)
+    advance(3, 3)
     advance(HEADS, 2)
-    advance(HEADS_END, 1)
+    send_document_parts()
     advance(HEADS_LAST, 2)
-    advance(2, 3)
-    send_document_parts()
     advance(OUT, 3)
     advance(HEADS_MID, 2)
+    complete(0)
     advance(SMALL, 2)
-    complete(4)
+    advance(4, 3)
     advance(HEADS, 3)
-    complete(3)
-    advance(5, 3)
     advance(HEADS_END, 2)
     advance(HEADS_LAST, 3)
     advance(HEADS_MID, 3)
+    advance(2, 3)
+    complete(OUT)
+    advance(SMALL, 3)
+    complete(3)
+    advance(HEADS_END, 3)
     input_grad(0)
-    advance(SMALL, 3)
-    complete(5)
-    complete(0)
-    advance(HEADS_END, 3)
     add_document_parts()
-    complete(HEADS_LAST)
+    complete(HEADS)
     sent_late()
     input_grad(1)
+    complete(HEADS_LAST)
     complete(HEADS_MID)
+    complete(4)
+    complete(SMALL)
     complete(2)
-    complete(SMALL)
-    complete(OUT)
-    complete(HEADS)
     complete(HEADS_END)
     for p in range(pairs):
         for part in range(2):

time: 94.3 us -> 93.7 us (level)
  no operation moved by 1% of the time
where the time goes in v5:
time: 93.7 us; the launch traced here: 93.5 us
  Pallas kernels  92.7 us (99%)
    pallas_call x1, Pallas kernels, body(): pl.pallas_call(functools.partial(layer_kernel, (n_batch, pairs, seq)), ou...  90.5 us
    pallas_call x1, Pallas kernels, body(): pl.pallas_call(functools.partial(finish_kernel, local), out_shape=(shape(...  2.19 us

profile of v5, /device:TPU:0, one launch (start us, length us, event | category | flops | bytes accessed | tf_op | source)
XLA Modules:
  0.0 93.5 jit_solution(12953438511172231323)
XLA Ops:
  0.7 90.5 %encoder_layer.1 = (bf16[576,768]{1,0:T(8,128)(2,1)S(1)}, bf16[576,768]{1,0:T(8,128)(2,1)S(1)}, f32[3,48,1536]{2,1,0:T(8,128)S(1)}, f32[16,128]{1,0:T(8,128)S(1)}, f32[16,128]{1,0:T(8,128)S(1)}) custom-call(bf16[576,768]{1,0:T(8,128)(2,1)} %tokens_hbm.1, bf16[576,768]{1,0:T(8,128)(2,1)} %cot_hbm.1, bf16[768,384]{1,0:T(8,128)(2,1)} %wq_hbm.1, ...), custom_call_target="tpu_custom_call" | custom-call | tf_op jit(solution)/shard_map/encoder_layer/pallas_call | solution.py:872
  91.2 2.2 %gradient_outputs.1 = (bf16[576,768]{1,0:T(8,128)(2,1)}, bf16[576,768]{1,0:T(8,128)(2,1)}, f32[2,768]{1,0:T(2,128)}, f32[48,384]{1,0:T(8,128)}, f32[24]{0:T(128)...) custom-call(bf16[576,768]{1,0:T(8,128)(2,1)S(1)} %get-tuple-element., ...), custom_call_target="tpu_custom_call" | custom-call | tf_op jit(solution)/shard_map/gradient_outputs/pallas_call | solution.py:921
